TPU v7x, 512 devices: a whole 4x8x8 slice. The times are simulated.
512 devices in a mesh: dp: 8 (over z), tm: 8 (over y_lo, core), height: 8 (over x, y_hi).
Axes of the slice: x: 4, y: 8 (y_hi: 2, y_lo: 4; y = y_hi * 4 + y_lo), z: 8, core: 2. Of those that a mesh axis runs over, the one named last changes fastest.
Arguments:
- clip_inputs: bfloat16 [8, 16, 16, 16, 512], P('dp', 'tm', 'height'), may hold values from -6 to 6
- conv_in_weight: bfloat16 [13824, 512], P(('tm', 'height'), 'dp'), may hold values from -0.0546875 to 0.0546875
- group_gain: bfloat16 [512], P('dp'), may hold values from 0.099609375 to 1.8984375
- group_bias: bfloat16 [512], P('dp'), may hold values from -3 to 3
- conv_out_weight: bfloat16 [27, 512, 16], P(None, 'dp'), may hold values from -0.109375 to 0.109375
- out_bias: float32 [16], replicated, may hold values from -3 to 3
- patch_weight: bfloat16 [64, 3072], replicated, may hold values from -1.5 to 1.5
- patch_bias: bfloat16 [3072], replicated, may hold values from -3 to 3
- qkv_weight: bfloat16 [3072, 6144], P(('tm', 'height'), 'dp'), may hold values from -0.109375 to 0.109375
- qkv_bias: bfloat16 [6144], P('dp'), may hold values from -3 to 3
- q_gain: bfloat16 [128], replicated, may hold values from 0.099609375 to 1.8984375
- k_gain: bfloat16 [128], replicated, may hold values from 0.099609375 to 1.8984375
- frame_pos: int32 [16], P('tm'), may hold values from 0 to 63
- row_pos: int32 [8], P('height'), may hold values from 0 to 127
Outputs:
- latents: float32 [8, 16, 16, 256], P('dp', 'tm', 'height')
- queries: bfloat16 [8, 16, 8, 8, 2048], P(None, 'tm', 'height', None, 'dp')
- keys: bfloat16 [8, 16, 8, 8, 2048], P(None, 'tm', 'height', None, 'dp')
- values: bfloat16 [8, 16, 8, 8, 2048], P(None, 'tm', 'height', None, 'dp')
All inputs are finite; a program needn't handle non-finite values.
Results may differ from a plain program's by a relative error of at most 0.01.
Values may be sent and summed in bfloat16 or wider, within the bound.
A program may use at most 64 MiB of HBM per device.

v0:
```python
import jax
import jax.numpy as jnp
from jax import lax
from jax.sharding import PartitionSpec as P

HD = 128
GROUPS = 32
TAPS = 27


norm_eps = 1e-06
latent_scale = 0.476986
rope_base = 256.0
time_dims = 16
row_dims = 56


def from_behind(value, axis, steps):
    count = lax.axis_size(axis)
    first, last = (max(0, -steps), min(count, count - steps))
    return lax.ppermute(value, axis, [(source, source + steps) for source in range(first, last)])


def padded_2(block, sides, width):
    for axis, dim in sides:
        count = lax.axis_size(axis)
        forward = [(i, i + 1) for i in range(count - 1)]
        backward = [(target, source) for source, target in forward]
        low = lax.ppermute(
            lax.slice_in_dim(block, block.shape[dim] - width, None, axis=dim), axis, forward
        )
        high = lax.ppermute(lax.slice_in_dim(block, 0, width, axis=dim), axis, backward)
        block = jnp.concatenate([low, block, high], axis=dim)
    return block


def repeat_first(block):
    return jnp.concatenate([block[:, :1], block[:, :1]], axis=1)


def time_join(block, earlier):
    start = jnp.where(lax.axis_index("tm") == 0, repeat_first(block), earlier)
    return jnp.concatenate([start, block], axis=1)


def rows_finish(grown):
    place = lax.axis_index("height")
    top = jnp.where(place == 0, grown[:, :, 1:2], grown[:, :, :1])
    bottom = jnp.where(place == lax.axis_size("height") - 1, grown[:, :, -2:-1], grown[:, :, -1:])
    inner = jnp.concatenate([top, grown[:, :, 1:-1], bottom], axis=2)
    return jnp.pad(inner, ((0, 0), (0, 0), (0, 0), (1, 1), (0, 0)), mode="edge")


def edges_before(block):
    earlier = from_behind(block, "tm", 1)
    longer = time_join(block, earlier)
    return rows_finish(padded_2(longer, (("height", 2),), 1))


def edges_norm(block):
    earlier = from_behind(block, "tm", 1)
    longer = time_join(block, earlier)
    return rows_finish(padded_2(longer, (("height", 2),), 1))


def convolve(padded, weight):
    clips = padded.shape[0]
    frames = padded.shape[1] - 2
    rows = padded.shape[2] - 2
    cols = padded.shape[3] - 2
    total = jnp.zeros((clips * frames * rows * cols, weight.shape[2]), jnp.float32)
    for shift_t in range(3):
        for shift_r in range(3):
            for shift_c in range(3):
                window = padded[
                    :,
                    shift_t : shift_t + frames,
                    shift_r : shift_r + rows,
                    shift_c : shift_c + cols,
                ]
                window = window.reshape(-1, padded.shape[4])
                total = total + jnp.dot(
                    window,
                    weight[9 * shift_t + 3 * shift_r + shift_c],
                    preferred_element_type=jnp.float32,
                )
    return total.reshape(clips, frames, rows, cols, weight.shape[2])


def section_freqs(dims):
    return jnp.power(rope_base, -jnp.arange(0, dims, 2, dtype=jnp.float32) / dims)


def rope_angles(tpos, hpos, width):
    frames = tpos.shape[0]
    rows = hpos.shape[0]
    cols = jnp.arange(width, dtype=jnp.float32)
    part_t = tpos[:, None, None, None] * section_freqs(time_dims)
    part_h = hpos[None, :, None, None] * section_freqs(row_dims)
    part_w = cols[None, None, :, None] * section_freqs(row_dims)
    shape = (frames, rows, width)
    return jnp.concatenate(
        [
            jnp.broadcast_to(part_t, shape + (time_dims // 2,)),
            jnp.broadcast_to(part_h, shape + (row_dims // 2,)),
            jnp.broadcast_to(part_w, shape + (row_dims // 2,)),
        ],
        axis=-1,
    )


def rotate(vectors, angles):
    pairs = vectors.reshape(vectors.shape[:-1] + (vectors.shape[-1] // 2, 2))
    first = pairs[..., 0]
    second = pairs[..., 1]
    cosine = jnp.cos(angles)[..., None, :]
    sine = jnp.sin(angles)[..., None, :]
    turned = jnp.stack([first * cosine - second * sine, first * sine + second * cosine], axis=-1)
    return turned.reshape(vectors.shape)


def rms_scale(vectors, gain):
    return (
        vectors
        * lax.rsqrt(jnp.mean(vectors * vectors, axis=-1, keepdims=True) + norm_eps)
        * gain.astype(jnp.float32)
    )


def shards(
    clip_inputs,
    conv_in_weight,
    group_gain,
    group_bias,
    conv_out_weight,
    out_bias,
    patch_weight,
    patch_bias,
    qkv_weight,
    qkv_bias,
    q_gain,
    k_gain,
    frame_pos,
    row_pos,
):
    channels = clip_inputs.shape[4]
    frames = clip_inputs.shape[1]
    rows = clip_inputs.shape[2]
    cols = clip_inputs.shape[3]
    padded = lax.all_gather(edges_before(clip_inputs), "dp", axis=0, tiled=True)
    clips = padded.shape[0]
    weight_in = lax.all_gather(conv_in_weight, ("tm", "height"), axis=0, tiled=True).reshape(
        TAPS, channels, -1
    )
    hidden = convolve(padded, weight_in)
    block_width = hidden.shape[4]
    group_width = channels // GROUPS
    local_groups = block_width // group_width
    grouped = hidden.reshape(clips, -1, local_groups, group_width)
    sums_local = jnp.sum(grouped, axis=(1, 3))
    squares_local = jnp.sum(grouped * grouped, axis=(1, 3))
    sums_all, squares_all = lax.psum((sums_local, squares_local), ("tm", "height"))
    count = float(
        frames * lax.axis_size("tm") * rows * lax.axis_size("height") * cols * group_width
    )
    mean = sums_all / count
    var = squares_all / count - mean * mean
    scaled = (grouped - mean[:, None, :, None]) * lax.rsqrt(var + norm_eps)[:, None, :, None]
    scaled = scaled.reshape(hidden.shape) * group_gain.astype(jnp.float32) + group_bias.astype(
        jnp.float32
    )
    normed = jax.nn.silu(scaled).astype(jnp.bfloat16)
    partial_latent = convolve(edges_norm(normed), conv_out_weight)
    own_sum = lax.psum_scatter(partial_latent, "dp", scatter_dimension=0, tiled=True)
    own_latent = (own_sum + out_bias) * latent_scale
    every_latent = lax.all_gather(own_latent.astype(jnp.bfloat16), "dp", axis=0, tiled=True)
    latent_dims = every_latent.shape[4]
    latents = own_latent.reshape(1, frames, rows, cols * latent_dims)
    tok_rows = rows // 2
    tok_cols = cols // 2
    patches = every_latent.reshape(clips, frames, tok_rows, 2, tok_cols, 2, latent_dims)
    patches = patches.transpose(0, 1, 2, 4, 3, 5, 6).reshape(-1, 4 * latent_dims)
    embedded = (
        jnp.dot(patches, patch_weight, preferred_element_type=jnp.float32)
        + patch_bias.astype(jnp.float32)
    ).astype(jnp.bfloat16)
    projected = jnp.dot(
        embedded,
        lax.all_gather(qkv_weight, ("tm", "height"), axis=0, tiled=True),
        preferred_element_type=jnp.float32,
    )
    projected = projected + qkv_bias.astype(jnp.float32)
    local_heads = qkv_weight.shape[1] // (3 * HD)
    projected = projected.reshape(clips, frames, tok_rows, tok_cols, local_heads, 3, HD)
    angles = rope_angles(frame_pos.astype(jnp.float32), row_pos.astype(jnp.float32), tok_cols)
    query = rotate(rms_scale(projected[..., 0, :], q_gain), angles)
    key = rotate(rms_scale(projected[..., 1, :], k_gain), angles)
    value = projected[..., 2, :]
    merged = (clips, frames, tok_rows, tok_cols, local_heads * HD)
    return (
        latents,
        query.reshape(merged).astype(jnp.bfloat16),
        key.reshape(merged).astype(jnp.bfloat16),
        value.reshape(merged).astype(jnp.bfloat16),
    )


def solution(mesh):
    placed = (
        P("dp", "tm", "height", None, None),
        P(("tm", "height"), "dp"),
        P("dp"),
        P("dp"),
        P(None, "dp", None),
        P(),
        P(),
        P(),
        P(("tm", "height"), "dp"),
        P("dp"),
        P(),
        P(),
        P("tm"),
        P("height"),
    )
    return jax.shard_map(
        shards,
        mesh=mesh,
        in_specs=placed,
        out_specs=(
            P("dp", "tm", "height", None),
            P(None, "tm", "height", None, "dp"),
            P(None, "tm", "height", None, "dp"),
            P(None, "tm", "height", None, "dp"),
        ),
        check_vma=False,
    )
```

profile of v0, /device:TPU:1, one launch (start us, length us, event | category | flops | bytes accessed | tf_op | source)
XLA Modules:
  0.0 745.8 jit_solution(8235028796349945031)
XLA Ops:
  7.2 0.7 all-gather.9.cloned.1.call-update
  8.0 0.9 copy.55
  8.9 4.6 collective-permute-start
  13.5 4.3 collective-permute-done
  18.1 3.6 collective-permute-start.1
  21.6 2.9 collective-permute-done.1
  24.9 1.3 collective-permute-start.2
  26.2 10.1 %collective-permute-done.2 = bf16[1,4,1,16,512]{4,2,3,1,0:T(2,128)(2,1)S(1)} collective-permute-done((bf16[1,4,1,16,512]{4,2,3,1,0:T(2,128)(2,1)S(1)}, bf16[1,4,1,16,512]{4,2,3,1,0:T(2,128)(2,1)S(1)}, u32[]{:S(2)}, u32[]{:S(2)}) %collective-permute-start.2) | collective-permute-done | bytes 65568 | tf_op jit(solution)/shard_map/ppermute | solution.py:32
  36.5 1.2 fusion.36
  37.9 164.6 %all-gather.9.cloned.1.call-done = bf16[64,216,64]{1,2,0:T(8,128)(2,1)} async-done(((bf16[1,216,64]{1,2,0:T(8,128)(2,1)}), bf16[64,216,64]{1,2,0:T(8,128)(2,1)}) %all-gather.9.cloned.1.call-update) | async-done | bytes 1769488 | tf_op jit(solution)/shard_map/all_gather | solution.py:152
  202.5 2.8 copy.59
  205.2 4.8 reshape.605
  210.0 41.4 %all-gather.5.cloned.1.call-done = bf16[8,4,4,18,512]{4,2,3,1,0:T(4,128)(2,1)} async-done(((bf16[1,4,4,18,512]{4,2,3,1,0:T(4,128)(2,1)}), bf16[8,4,4,18,512]{4,2,3,1,0:T(4,128)(2,1)}) %all-gather.5.cloned.1.call-update) | async-done | bytes 2359312 | tf_op jit(solution)/shard_map/all_gather | solution.py:150
  251.5 8.3 %fusion.139 = (bf16[8,2,2,16,512]{4,2,3,1,0:T(2,128)(2,1)S(1)}, bf16[8,2,2,16,512]{4,2,3,1,0:T(2,128)(2,1)S(1)}, bf16[8,2,2,16,512]{4,2,3,1,0:T(2,128)(2,1)S(1)}...) fusion(bf16[8,4,4,18,512]{4,2,3,1,0:T(4,128)(2,1)} %all-gather., ...), kind=kLoop, calls=%fused_computation.236 | loop fusion | bytes 8388608 | tf_op jit(solution)/shard_map/slice | solution.py:75
  260.4 1.4 copy-done.1
  261.8 10.9 %fusion.138 = (bf16[8,2,2,16,512]{4,2,3,1,0:T(2,128)(2,1)S(1)}, bf16[8,2,2,16,512]{4,2,3,1,0:T(2,128)(2,1)S(1)}, bf16[8,2,2,16,512]{4,2,3,1,0:T(2,128)(2,1)S(1)}...) fusion(bf16[8,4,4,18,512]{4,2,3,1,0:T(4,128)(2,1)S(1)} %copy-done.1), kind=kLoop, calls=%fused_computation.235 | loop fusion | bytes 19922944 | tf_op jit(solution)/shard_map/slice | solution.py:75
  274.3 1.2 copy-done.3
  283.6 179.1 %all-reduce = (f32[8,4]{0,1:T(4,128)S(1)}, f32[8,4]{0,1:T(4,128)S(1)}) all-reduce(f32[8,4]{0,1:T(4,128)S(1)} %get-tuple-element.17, f32[8,4]{0,1:T(4,128)S(1)} %get-tuple-element.16), channel_id=1, replica_groups=mesh['dp'=8,'tm'=8,'height'=8] {'tm','height'}, use_global_device_ids=true, to_apply=%region_3.4 | all-reduce | flops 64 | bytes 512 | tf_op jit(solution)/shard_map/psum | solution.py:162
  463.3 1.9 collective-permute-start.3
  465.2 1.9 collective-permute-done.3
  467.2 1.3 collective-permute-start.4
  468.8 2.7 collective-permute-done.4
  471.6 1.5 collective-permute-start.5
  473.1 9.8 %collective-permute-done.5 = bf16[8,4,1,16,64]{4,3,2,1,0:T(8,128)(2,1)S(1)} collective-permute-done((bf16[8,4,1,16,64]{4,3,2,1,0:T(8,128)(2,1)S(1)}, bf16[8,4,1,16,64]{4,3,2,1,0:T(8,128)(2,1)S(1)}, u32[]{:S(2)}, u32[]{:S(2)}) %collective-permute-start.5) | collective-permute-done | bytes 65568 | tf_op jit(solution)/shard_map/ppermute | solution.py:32
  483.0 0.4 fusion.16
  483.5 0.6 fusion.140
  488.8 0.8 copy.106
  489.7 0.5 all-gather.7.cloned.1.call-update
  491.8 35.3 %reduce-scatter.2.cloned.1.call-done = f32[1,2,2,16,16]{4,3,2,1,0:T(8,128)} async-done(((f32[8,2,2,16,16]{4,3,2,1,0:T(8,128)}), f32[1,2,2,16,16]{4,3,2,1,0:T(8,128)}) %reduce-scatter.2.cloned.1.call-update) | async-done | bytes 4112 | tf_op jit(solution)/shard_map/reduce_scatter | solution.py:174
  527.1 0.8 fusion.136
  527.9 18.5 %all_gather.14 = bf16[8,2,2,16,16]{4,3,2,1,0:T(8,128)(2,1)S(1)} all-gather(bf16[1,2,2,16,16]{4,3,2,1,0:T(8,128)(2,1)S(1)} %get-tuple-element.20), channel_id=1, replica_groups=mesh['dp'=8,'tm'=8,'height'=8] {'dp'}, dimensions={0}, use_global_device_ids=true | all-gather | bytes 18432 | tf_op jit(solution)/shard_map/all_gather | solution.py:176
  546.7 0.7 reshape.598
  547.4 174.8 %all-gather.7.cloned.1.call-done = bf16[3072,768]{1,0:T(8,128)(2,1)} async-done(((bf16[48,768]{1,0:T(8,128)(2,1)}), bf16[3072,768]{1,0:T(8,128)(2,1)}) %all-gather.7.cloned.1.call-update) | async-done | bytes 4718608 | tf_op jit(solution)/shard_map/all_gather | solution.py:189
  722.2 3.4 fusion.10
  725.6 0.6 fusion.43
  726.3 0.7 copy.134
  727.2 2.0 copy.135
  729.2 1.8 multiply_reduce_fusion
  731.2 1.3 copy-done.2
  732.9 0.6 multiply_subtract_fusion
  733.4 0.4 copy.101
  733.8 0.4 copy.102
  734.2 0.8 copy.103
  735.0 1.3 copy.105
  736.3 0.4 copy.97
  736.7 0.4 copy.98
  737.1 0.8 copy.99
  737.9 1.3 copy.104
  (167 shorter events, 18.9 us)
Async XLA Ops:
  7.2 715.0 %copy-start = (bf16[64,3072]{1,0:T(8,128)(2,1)S(1)}, bf16[64,3072]{1,0:T(8,128)(2,1)}, u32[]{:S(2)}) copy-start(bf16[64,3072]{1,0:T(8,128)(2,1)} %param.20) | copy-start | bytes 1179652
  7.2 30.7 %copy-start.10 = (bf16[64]{0:T(256)(128)(2,1)S(1)}, bf16[64]{0:T(256)(128)(2,1)}, u32[]{:S(2)}) copy-start(bf16[64]{0:T(256)(128)(2,1)} %param.16) | copy-start | bytes 388
  7.2 30.7 %copy-start.11 = (bf16[64]{0:T(256)(128)(2,1)S(1)}, bf16[64]{0:T(256)(128)(2,1)}, u32[]{:S(2)}) copy-start(bf16[64]{0:T(256)(128)(2,1)} %param.17) | copy-start | bytes 388
  7.2 195.3 %all-gather.9.cloned.1.call-start = ((), (), s32[]{:S(2)}) async-start(), calls=%async_computation.4 | async-start | bytes 2129920 | tf_op jit(solution)/shard_map/all_gather | solution.py:152
  7.9 243.5 %all-gather.5.cloned.1.call-start = ((), (), s32[]{:S(2)}) async-start(), calls=%async_computation.1 | async-start | bytes 2654208 | tf_op jit(solution)/shard_map/all_gather | solution.py:150
  8.9 8.9 %collective-permute-start = (bf16[1,2,2,16,512]{4,2,3,1,0:T(2,128)(2,1)S(1)}, bf16[1,2,2,16,512]{4,2,3,1,0:T(2,128)(2,1)S(1)}, u32[]{:S(2)}, u32[]{:S(2)}) collective-permute-start(bf16[1,2,2,16,512]{4,2,3,1,0:T(2,128)(2,1)S(1)} %copy.55), channel_id=1, source_target_pairs={{0,8},{8,16},{16,24},{24,32},{32,40},{40,48},{48,56},{1,9},{9,17},... | collective-permute-start | bytes 196616 | tf_op jit(solution)/shard_map/ppermute | solution.py:21
  18.1 6.5 collective-permute-start.1
  24.9 11.4 %collective-permute-start.2 = (bf16[1,4,1,16,512]{4,2,3,1,0:T(2,128)(2,1)S(1)}, bf16[1,4,1,16,512]{4,2,3,1,0:T(2,128)(2,1)S(1)}, u32[]{:S(2)}, u32[]{:S(2)}) collective-permute-start(bf16[1,4,1,16,512]{4,2,3,1,0:T(2,128)(2,1)S(1)} %get-tuple-element.25), channel_id=1, source_target_pairs={{1,0},{2,1},{3,2},{4,3},{5,4},{6,5},{7,6},{9,8},{10,9},{11,10},{12... | collective-permute-start | bytes 196616 | tf_op jit(solution)/shard_map/ppermute | solution.py:32
  37.8 489.3 %reduce-scatter.2.cloned.1.call-start = ((), (), s32[]{:S(2)}) async-start(), calls=%async_computation.2 | async-start | bytes 294912 | tf_op jit(solution)/shard_map/reduce_scatter | solution.py:174
  260.1 1.7 copy-start.1
  274.0 1.5 copy-start.3
  463.3 3.9 collective-permute-start.3
  467.2 4.3 collective-permute-start.4
  471.6 11.3 %collective-permute-start.5 = (bf16[8,4,1,16,64]{4,3,2,1,0:T(8,128)(2,1)S(1)}, bf16[8,4,1,16,64]{4,3,2,1,0:T(8,128)(2,1)S(1)}, u32[]{:S(2)}, u32[]{:S(2)}) collective-permute-start(bf16[8,4,1,16,64]{4,3,2,1,0:T(8,128)(2,1)S(1)} %get-tuple-element.23), channel_id=1, source_target_pairs={{1,0},{2,1},{3,2},{4,3},{5,4},{6,5},{7,6},{9,8},{10,9},{11,10},{12... | collective-permute-start | bytes 196616 | tf_op jit(solution)/shard_map/ppermute | solution.py:32
  483.5 0.9 copy-start.4
  486.8 3.5 copy-start.5
  487.0 3.3 copy-start.6
  487.0 3.3 copy-start.7
  487.0 3.5 copy-start.8
  487.0 3.6 copy-start.12
  487.1 40.0 %copy-start.9 = (f32[16]{0:T(128)S(1)}, f32[16]{0:T(128)}, u32[]{:S(2)}) copy-start(f32[16]{0:T(128)} %param.19) | copy-start | bytes 196
  489.7 232.5 %all-gather.7.cloned.1.call-start = ((), (), s32[]{:S(2)}) async-start(), calls=%async_computation.3 | async-start | bytes 4792320 | tf_op jit(solution)/shard_map/all_gather | solution.py:189
  731.0 1.6 copy-start.2
Sparse Core Ops, SparseCore 0:
  10.1 192.2 all-gather.8
  204.5 46.8 all-gather.4
  489.8 37.2 reduce-scatter.1
  529.3 192.8 all-gather.6
where the time goes:
time: 752 us; the launch traced here: 746 us
  waiting for transfers between devices  449 us (60%)
  blocking collectives  198 us (26%)
  local copies, waits for them, and re-layouts  47.1 us (6%)
  matrix products  15.3 us (2%)
  between operations  15.2 us (2%)
  starting transfers between devices  14.3 us (2%)
    psum x1, blocking collectives, shards(): lax.psum((sums_local, squares_local), ('tm', 'height'))  179 us
    all_gather x1, waiting for transfers between devices, shards(): lax.all_gather(qkv_weight, ('tm', 'height'), axis=0, tiled=True)  175 us
    all_gather x1, waiting for transfers between devices, shards(): lax.all_gather(conv_in_weight, ('tm', 'height'), axis=0, tiled=True)  165 us
    all_gather x1, waiting for transfers between devices, shards(): padded = lax.all_gather(edges_before(clip_inputs), 'dp', axis=0, tiled=True)  41.4 us
    reduce_scatter x1, waiting for transfers between devices, shards(): lax.psum_scatter(partial_latent, 'dp', scatter_dimension=0, tiled=True)  35.3 us
    ppermute x2, waiting for transfers between devices, padded_2(): lax.ppermute(lax.slice_in_dim(block, 0, width, axis=dim), axis, backward)  19.9 us
    slice x4, local copies, waits for them, and re-layouts, convolve(): padded[:, shift_t:shift_t + frames, shift_r:shift_r + rows, shift_c:shift...  19.8 us
    all_gather x1, blocking collectives, shards(): lax.all_gather(own_latent.astype(jnp.bfloat16), 'dp', axis=0, tiled=True)  18.5 us
  transfers between devices with their start and end apart: 10, of which 10 were waited for; matrix products, arithmetic and copies ran while one was open for 2% of the time, Pallas kernels for 0%

commit v1 on v0

v1 whole, which is shorter than its diff:
```python
import math

import jax
import jax.numpy as jnp
from jax import lax
from jax.experimental import pallas as pl
from jax.experimental.pallas import tpu as pltpu
from jax.sharding import PartitionSpec as P

HD = 128
GROUPS = 32
TAPS = 27
N = 8

norm_eps = 1e-06
latent_scale = 0.476986
rope_base = 256.0
time_dims = 16
row_dims = 56

F32 = jnp.float32
BF16 = jnp.bfloat16
MESH = pl.DeviceIdType.MESH

SLOT_STEP = (0, -1, 1, -2, 2, -3, 3, -4)

NT = (((1,), (1,)), ((), ()))


def iota(shape, dim):
    return lax.broadcasted_iota(jnp.int32, shape, dim)


def chunk(ref, which):
    if which == 0:
        return ref.at[pl.ds(2, 2), pl.ds(1, 2)]
    if which == 1:
        return ref.at[pl.ds(0, 2), pl.ds(1, 2)]
    if which == 2:
        return ref.at[pl.ds(0, 4), pl.ds(0, 1)]
    return ref.at[pl.ds(0, 4), pl.ds(3, 1)]


def kernel(
    x_ref,
    wi_ref,
    gg_ref,
    gb_ref,
    wo_ref,
    ob_ref,
    pw_ref,
    pb_ref,
    qw_ref,
    qb_ref,
    qg_ref,
    kg_ref,
    fp_ref,
    rp_ref,
    lat_ref,
    q_ref,
    k_ref,
    v_ref,
    xe,
    wg,
    bt,
    ht,
    w2,
    place,
    wp,
    wr,
    wsum,
    wrh,
    wth,
    wf,
    wcc,
    st,
    str_t,
    str_h,
    outs,
    rz,
    ext,
    rh,
    pb,
    trig,
    zr_s,
    zr_r,
    zl_s,
    zl_r,
    ha_s,
    ha_r,
    wx_s,
    wx_r,
    yr_s,
    yr_r,
    yl_s,
    yl_r,
    co_s,
    co_r,
    wc_s,
    wc_r,
    ss_s,
    ss_r,
    rz_s,
    rz_r,
    rh_s,
    rh_r,
    pb_s,
    pb_r,
):
    z = lax.axis_index("dp")
    tm = lax.axis_index("tm")
    hh = lax.axis_index("height")
    core = lax.rem(tm, 2)
    y_lo = tm // 2
    x = hh // 2
    y_hi = lax.rem(hh, 2)
    y = y_hi * 4 + y_lo

    def at_y(where):
        return (z, lax.rem(where, 4) * 2 + core, x * 2 + where // 4)

    def remote(src, dst, send, recv, device):
        return pltpu.make_async_remote_copy(
            src_ref=src,
            dst_ref=dst,
            send_sem=send,
            recv_sem=recv,
            device_id=device,
            device_id_type=MESH,
        )

    z_up = (lax.rem(z + 1, N), tm, hh)
    z_down = (lax.rem(z + N - 1, N), tm, hh)
    y_up = at_y(lax.rem(y + 1, N))
    y_down = at_y(lax.rem(y + N - 1, N))
    other_core = (z, tm + 1 - 2 * core, hh)

    barrier = pltpu.get_barrier_semaphore()

    def greet(k, _):
        for device in (
            (lax.rem(z + k, N), tm, hh),
            (z, lax.rem(tm + k, N), hh),
            (z, tm, lax.rem(hh + k, N)),
        ):
            pl.semaphore_signal(barrier, inc=1, device_id=device, device_id_type=MESH)
        return 0

    lax.fori_loop(1, N, greet, 0)
    for dt in (1, N - 1):
        for dh in (1, N - 1):
            device = (z, lax.rem(tm + dt, N), lax.rem(hh + dh, N))
            pl.semaphore_signal(barrier, inc=1, device_id=device, device_id_type=MESH)
    for device in (y_up, y_down):
        pl.semaphore_signal(barrier, inc=1, device_id=device, device_id_type=MESH)

    eye = (iota((64, 64), 0) == iota((64, 64), 1)).astype(BF16)
    shard = lax.dot_general(eye, wi_ref[...], NT, preferred_element_type=F32)
    wg[y, core, x] = jnp.zeros((64, 256), BF16)
    wg[y, core, x, :, pl.ds(0, 216)] = shard.astype(BF16)

    d = tm * N + hh
    tile = jnp.minimum(48 * d // 128, 22)
    shift = 48 * d - 128 * tile
    window = pl.ds(pl.multiple_of(tile * 128, 128), 256)
    embed = jnp.concatenate(
        [pw_ref[:, window].astype(F32), jnp.broadcast_to(pb_ref[:, window].astype(F32), (8, 256))],
        axis=0,
    )
    embed = pltpu.roll(embed, lax.rem(256 - shift, 256), 1)[:, :48].astype(BF16)
    part = jnp.dot(embed, qw_ref[...], preferred_element_type=F32)
    for row in range(9):
        for lane in range(6):
            wp[row * 6 + lane] = part[8 * row : 8 * row + 8, 128 * lane : 128 * lane + 128]
    wp[pl.ds(54, 10)] = jnp.zeros((10, 8, 128), F32)

    pl.semaphore_wait(barrier, 27)

    def z_right(step, part):
        src = chunk(xe.at[SLOT_STEP.index(-step + 1) if step > 1 else 0], part)
        if step == 1 and part == 0:
            src = x_ref
        return remote(
            src,
            chunk(xe.at[SLOT_STEP.index(-step)], part),
            zr_s.at[step - 1, part],
            zr_r.at[step - 1, part],
            z_up,
        )

    def z_left(step, part):
        src = chunk(xe.at[SLOT_STEP.index(step - 1)], part)
        if step == 1 and part == 0:
            src = x_ref
        return remote(
            src,
            chunk(xe.at[SLOT_STEP.index(step)], part),
            zl_s.at[step - 1, part],
            zl_r.at[step - 1, part],
            z_down,
        )

    own = xe.at[0]
    has_next = tm < N - 1
    has_last = tm > 0
    has_up = hh < N - 1
    has_down = hh > 0
    next_tm = lax.rem(tm + 1, N)
    up_h = lax.rem(hh + 1, N)
    down_h = lax.rem(hh + N - 1, N)
    row_0 = x_ref.at[:, pl.ds(0, 1)]
    row_1 = x_ref.at[:, pl.ds(1, 1)]
    halos = (
        (x_ref, own.at[pl.ds(0, 2), pl.ds(1, 2)], (z, next_tm, hh), has_next, has_last),
        (row_0, own.at[pl.ds(2, 2), pl.ds(3, 1)], (z, tm, down_h), has_down, has_up),
        (row_1, own.at[pl.ds(2, 2), pl.ds(0, 1)], (z, tm, up_h), has_up, has_down),
        (
            row_0,
            own.at[pl.ds(0, 2), pl.ds(3, 1)],
            (z, next_tm, down_h),
            has_next & has_down,
            has_last & has_up,
        ),
        (
            row_1,
            own.at[pl.ds(0, 2), pl.ds(0, 1)],
            (z, next_tm, up_h),
            has_next & has_up,
            has_last & has_down,
        ),
    )

    def halo_copy(i):
        src, dst, device, _, _ = halos[i]
        return remote(src, dst, ha_s.at[i], ha_r.at[i], device)

    z_right(1, 0).start()
    z_left(1, 0).start()
    for i in range(5):
        pl.when(halos[i][3])(lambda i=i: halo_copy(i).start())

    def x_copy(k):
        return remote(
            wg.at[y, core, x],
            wg.at[y, core, x],
            wx_s.at[k],
            wx_r.at[k],
            (z, tm, lax.rem(hh + 2 * k, N)),
        )

    def x_wait(k):
        from_x = lax.rem(x + 4 - k, 4)
        remote(
            wg.at[y, core, x],
            wg.at[y, core, from_x],
            wx_s.at[k],
            wx_r.at[k],
            (z, tm, lax.rem(hh + 2 * k, N)),
        ).wait_recv()

    for k in range(1, 4):
        x_copy(k).start()

    def fold_1(k):
        to = lax.rem(tm + k, N)
        return remote(
            wp.at[pl.ds(8 * to, 8)], wr.at[k], wc_s.at[0, k], wc_r.at[0, k], (z, to, hh)
        )

    def fold_2(k):
        to = lax.rem(hh + k, N)
        return remote(wsum.at[to], wrh.at[k], wc_s.at[1, k], wc_r.at[1, k], (z, tm, to))

    def fold_3(k, source):
        to = lax.rem(hh + k, N)
        return remote(
            wth.at[hh], wth.at[source], wc_s.at[2, k], wc_r.at[2, k], (z, tm, to)
        )

    def fold_4(k, source):
        to = lax.rem(tm + k, N)
        return remote(
            wf.at[tm], wf.at[source], wc_s.at[3, k], wc_r.at[3, k], (z, to, hh)
        )

    def each(fn):
        def body(k, _):
            fn(k)
            return 0

        lax.fori_loop(1, N, body, 0)

    each(lambda k: fold_1(k).start())

    xe[0, 2:4, 1:3] = x_ref[...]

    eye16 = (iota((16, 16), 0) == iota((16, 16), 1)).astype(BF16)
    for ij in range(9):
        w2[16 * ij : 16 * ij + 16] = jnp.concatenate(
            [
                lax.dot_general(eye16, wo_ref[3 * ij + l], NT, preferred_element_type=F32)
                for l in range(3)
            ],
            axis=1,
        ).astype(BF16)

    for k in range(1, 4):
        x_wait(k)

    def y_right(step):
        from_y = lax.rem(y + N - step + 1, N)
        return remote(
            wg.at[from_y, core], wg.at[from_y, core], yr_s.at[step - 1], yr_r.at[step - 1], y_up
        )

    def y_right_wait(step):
        from_y = lax.rem(y + N - step, N)
        remote(
            wg.at[from_y, core], wg.at[from_y, core], yr_s.at[step - 1], yr_r.at[step - 1], y_up
        ).wait_recv()

    def y_left(step):
        from_y = lax.rem(y + step - 1, N)
        return remote(
            wg.at[from_y, core], wg.at[from_y, core], yl_s.at[step - 1], yl_r.at[step - 1], y_down
        )

    def y_left_wait(step):
        from_y = lax.rem(y + step, N)
        remote(
            wg.at[from_y, core], wg.at[from_y, core], yl_s.at[step - 1], yl_r.at[step - 1], y_down
        ).wait_recv()

    def core_copy(slot):
        from_y = lax.rem(y + N + SLOT_STEP[slot], N)
        return remote(
            wg.at[from_y, core], wg.at[from_y, core], co_s.at[slot], co_r.at[slot], other_core
        )

    def core_wait(slot):
        from_y = lax.rem(y + N + SLOT_STEP[slot], N)
        other = 1 - core
        remote(
            wg.at[from_y, other], wg.at[from_y, other], co_s.at[slot], co_r.at[slot], other_core
        ).wait_recv()

    y_right(1).start()
    y_left(1).start()
    core_copy(0).start()

    def halo_wait(i, fill):
        pl.when(halos[i][4])(lambda: halo_copy(i).wait_recv())
        if fill is not None:
            pl.when(jnp.logical_not(halos[i][4]))(fill)

    def first_frames():
        first = x_ref[0:1]
        xe[0, 0:1, 1:3] = first
        xe[0, 1:2, 1:3] = first

    halo_wait(0, first_frames)
    z_right(1, 1).start()
    z_left(1, 1).start()
    for i in range(1, 5):
        halo_wait(i, None)

    def first_corner(row):
        def fill():
            edge = xe[0, 2:3, row : row + 1]
            xe[0, 0:1, row : row + 1] = edge
            xe[0, 1:2, row : row + 1] = edge

        return fill

    @pl.when(jnp.logical_not(has_last) & has_down)
    def _():
        first_corner(0)()

    @pl.when(jnp.logical_not(has_last) & has_up)
    def _():
        first_corner(3)()

    @pl.when(jnp.logical_not(has_down))
    def _():
        xe[0, :, 0:1] = xe[0, :, 1:2]

    @pl.when(jnp.logical_not(has_up))
    def _():
        xe[0, :, 3:4] = xe[0, :, 2:3]

    for part in (2, 3):
        z_right(1, part).start()
        z_left(1, part).start()

    def ring_step(step):
        for part in range(4):
            z_right(step, part).wait_recv()
            z_right(step + 1, part).start()
            z_left(step, part).wait_recv()
            if step < 3:
                z_left(step + 1, part).start()

    def weight_step(step):
        y_right_wait(step)
        if step < 4:
            y_right(step + 1).start()
        core_copy(2 * step - 1).start()
        if step < 4:
            y_left_wait(step)
            if step < 3:
                y_left(step + 1).start()
            core_copy(2 * step).start()

    ring_step(1)
    weight_step(1)

    each(lambda k: fold_1(k).wait_recv())
    total = wp[pl.ds(8 * tm, 8)]
    for k in range(1, N):
        total = total + wr[k]
    wsum[...] = total
    each(lambda k: fold_2(k).start())

    ring_step(2)
    weight_step(2)

    each(lambda k: fold_2(k).wait_recv())
    tile_sum = wsum[hh]
    for k in range(1, N):
        tile_sum = tile_sum + wrh[k]
    wth[hh] = tile_sum
    each(lambda k: fold_3(k, hh).start())

    ring_step(3)
    weight_step(3)

    each(lambda k: fold_3(k, lax.rem(hh + N - k, N)).wait_recv())
    wf[tm] = wth[...]
    each(lambda k: fold_4(k, tm).start())

    lane = iota((128, 512), 1)
    row = iota((128, 512), 0)
    s_at = (lane >> 6) & 3
    q_at = (lane >> 4) & 3
    f_at = (row >> 5) & 1
    r_at = (row >> 4) & 1
    in_frame = (s_at == f_at + 2) | ((tm == 0) & (s_at < 2) & (f_at == 0))
    in_row = (
        (q_at == r_at + 1)
        | ((hh == 0) & (q_at == 0) & (r_at == 0))
        | ((hh == N - 1) & (q_at == 3) & (r_at == 1))
    )
    same = ((lane & 15) == (row & 15)) & ((lane >> 8) == (row >> 6))
    place[...] = jnp.where(in_frame & in_row & same, 1.0, 0.0).astype(BF16)

    entry = iota((16, 128), 1) >> 1
    token = iota((16, 128), 0)
    is_frame = entry < 8
    is_row = entry < 36
    start = jnp.where(is_frame, 0, jnp.where(is_row, 8, 36))
    width = jnp.where(is_frame, float(time_dims), float(row_dims))
    power = 2.0 * (entry - start).astype(F32) / width
    freq = jnp.exp(power * (-math.log(rope_base)))
    frame_at = jnp.where(token < 8, fp_ref[0].astype(F32), fp_ref[1].astype(F32))
    spot = jnp.where(
        is_frame,
        frame_at,
        jnp.where(is_row, rp_ref[0].astype(F32), (token & 7).astype(F32)),
    )
    angle = spot * freq
    trig[0] = jnp.cos(angle)
    odd = (iota((16, 128), 1) & 1) == 1
    sine = jnp.sin(angle)
    trig[1] = jnp.where(odd, sine, -sine)

    weight_step(4)
    for slot in range(N):
        core_wait(slot)

    def shard_of(index):
        t, h = index // N, index % N
        return wg[(h % 2) * 4 + t // 2, t % 2, h // 2]

    for tile in range(4 * TAPS):
        source, first = (128 * tile) // 216, (128 * tile) % 216
        count = min(128, 216 - first)
        value = shard_of(source)[:, first : first + count]
        if count < 128:
            value = jnp.concatenate([value, shard_of(source + 1)[:, : 128 - count]], axis=1)
        tap = tile // 4
        ij, l = tap // 3, tap % 3
        at = 128 * (tile % 4)
        bt[ij, 64 * l : 64 * l + 64, at : at + 128] = value

    col = iota((64, 128), 1) & 15

    def conv_pair(pair):
        total = jnp.zeros((192, 128), F32)
        for ij in range(9):
            i, j = ij // 3, ij % 3
            block = xe[2 * pair : 2 * pair + 2, i : i + 2, j : j + 2].reshape(128, 512)
            total = total + lax.dot_general(bt[ij], block, NT, preferred_element_type=F32)
        left, mid, right = total[:64], total[64:128], total[128:]
        left = jnp.where(col == 0, left, pltpu.roll(left, 1, 1))
        right = jnp.where(col == 15, right, pltpu.roll(right, 127, 1))
        ht[pair] = left + mid + right

    for pair in range(3):
        conv_pair(pair)
    for part in range(4):
        z_right(4, part).wait_recv()
    conv_pair(3)

    stat_lane = iota((8, 128), 1)
    compact = jnp.zeros((8, 128), F32)
    for pair in range(4):
        value = ht[pair]
        sums = jnp.sum(value.reshape(4, 16, 128), axis=1)
        squares = jnp.sum((value * value).reshape(4, 16, 128), axis=1)
        both = jnp.concatenate([sums, squares], axis=0)
        low = jnp.sum(jnp.where(stat_lane < 64, both, 0.0), axis=1, keepdims=True)
        high = jnp.sum(jnp.where(stat_lane >= 64, both, 0.0), axis=1, keepdims=True)
        compact = jnp.where(stat_lane == pair, low, compact)
        compact = jnp.where(stat_lane == 64 + pair, high, compact)
    st[0] = compact

    def stat_1(k):
        to = lax.rem(tm + k, N)
        return remote(st.at[0], str_t.at[k], ss_s.at[0, k], ss_r.at[0, k], (z, to, hh))

    def stat_2(k):
        to = lax.rem(hh + k, N)
        return remote(st.at[1], str_h.at[k], ss_s.at[1, k], ss_r.at[1, k], (z, tm, to))

    each(lambda k: stat_1(k).start())

    each(lambda k: fold_4(k, lax.rem(tm + N - k, N)).wait_recv())

    each(lambda k: stat_1(k).wait_recv())
    for k in range(1, N):
        compact = compact + str_t[k]
    st[1] = compact
    each(lambda k: stat_2(k).start())

    for lane_tile in range(6):
        for pair in range(4):
            tiles = [12 * pair + lane_tile, 12 * pair + 6 + lane_tile]
            value = jnp.concatenate([wf[t // 8, t % 8] for t in tiles], axis=0)
            high = value.astype(BF16)
            low = (value - high.astype(F32)).astype(BF16)
            at = slice(128 * lane_tile, 128 * lane_tile + 128)
            wcc[16 * pair : 16 * pair + 16, at] = high
            wcc[64 + 16 * pair : 64 + 16 * pair + 16, at] = low

    diag = iota((64, 64), 0) == iota((64, 64), 1)
    gain = jnp.sum(jnp.where(diag, gg_ref[...].astype(F32), 0.0), axis=1, keepdims=True)
    bias = jnp.sum(jnp.where(diag, gb_ref[...].astype(F32), 0.0), axis=1, keepdims=True)
    diag = iota((16, 16), 0) == iota((16, 16), 1)
    out_bias = jnp.sum(jnp.where(diag, ob_ref[...], 0.0), axis=1, keepdims=True)

    each(lambda k: stat_2(k).wait_recv())
    for k in range(1, N):
        compact = compact + str_h[k]
    count = float(16 * 16 * 16 * 16)
    average = compact / count
    mean = average
    var = pltpu.roll(average, 4, 0) - mean * mean
    inv = lax.rsqrt(var + norm_eps)

    wide = iota((16, 512), 1)
    t_at = (wide >> 6) & 3
    u_at = (wide >> 4) & 3
    lane_128 = iota((8, 128), 1)

    def spread(value, pair):
        lanes = jnp.where(
            lane_128 < 64,
            jnp.broadcast_to(value[:, pair : pair + 1], (8, 128)),
            jnp.broadcast_to(value[:, 64 + pair : 65 + pair], (8, 128)),
        )
        return jnp.concatenate(
            [jnp.broadcast_to(lanes[g : g + 1], (16, 128)) for g in range(4)], axis=0
        )

    def rz_copy(slot):
        to = lax.rem(z + N + SLOT_STEP[slot], N)
        return remote(outs.at[slot], rz.at[slot], rz_s.at[slot], rz_r.at[slot], (to, tm, hh))

    for pair in (3, 2, 1, 0):
        scale = spread(inv, pair) * gain
        offset = bias - spread(mean, pair) * scale
        value = ht[pair] * scale + offset
        value = value / (1.0 + jnp.exp(-value))
        left = jnp.where(col == 0, value, pltpu.roll(value, 1, 1))
        right = jnp.where(col == 15, value, pltpu.roll(value, 127, 1))
        stacked = jnp.concatenate([left, value, right], axis=0).astype(BF16)
        spots = jnp.dot(stacked, place[...], preferred_element_type=F32).astype(BF16)
        taps = jnp.dot(w2[...], spots, preferred_element_type=F32)
        total = jnp.zeros((16, 512), F32)
        for ij in range(9):
            i, j = ij // 3, ij % 3
            move = (16 * (1 - j) - 64 * i) % 512
            moved = taps[16 * ij : 16 * ij + 16]
            if move:
                moved = pltpu.roll(moved, move, 1)
            valid = t_at <= 3 - i
            if j == 0:
                valid = valid & (u_at >= 1)
            if j == 2:
                valid = valid & (u_at <= 2)
            total = total + jnp.where(valid, moved, 0.0)
        outs[2 * pair] = total[:, :256]
        outs[2 * pair + 1] = total[:, 256:]
        for slot in (2 * pair + 1, 2 * pair):
            if slot:
                rz_copy(slot).start()

    for i in range(5):

        @pl.when(jnp.logical_not(halos[i][4]))
        def _(i=i):
            rh[i] = jnp.zeros((16, 128), F32)

    total = outs[0]
    for slot in range(1, N):
        rz_copy(slot).wait_recv()
        total = total + rz[slot]
    ext[0] = total[:, :128]
    ext[1] = total[:, 128:]

    def rh_copy(i):
        return remote(
            ext.at[1 if i in (0, 3, 4) else 0],
            rh.at[i],
            rh_s.at[i],
            rh_r.at[i],
            halos[i][2],
        )

    for i in range(5):
        pl.when(halos[i][3])(lambda i=i: rh_copy(i).start())
    for i in range(5):
        pl.when(halos[i][4])(lambda i=i: rh_copy(i).wait_recv())

    narrow = iota((16, 128), 1)
    u_at = (narrow >> 4) & 3
    inside = (u_at == 1) | (u_at == 2)
    latent = jnp.where(inside, total[:, :128] + rh[0], 0.0)
    latent = latent + jnp.where(u_at == 2, pltpu.roll(rh[1] + rh[3], 32, 1), 0.0)
    latent = latent + jnp.where(u_at == 1, pltpu.roll(rh[2] + rh[4], 96, 1), 0.0)
    latent = (latent + out_bias) * latent_scale

    lane = iota((128, 128), 1)
    group = (iota((128, 128), 0) >> 4) & 3
    keep = (((lane >> 4) & 3) == (group >> 1) + 1) & ((lane & 1) == (group & 1))
    rounded = latent.astype(BF16).astype(F32)
    many = jnp.where(keep, jnp.concatenate([rounded] * 8, axis=0), 0.0).astype(BF16)
    lane = iota((16, 128), 1)
    row = iota((16, 128), 0)
    pick = ((lane >> 6) == (row >> 3)) & (((lane & 15) >> 1) == (row & 7))
    pick = jnp.where(pick, 1.0, 0.0).astype(BF16)
    pb[z] = lax.dot_general(pick, many, NT, preferred_element_type=F32).astype(BF16)

    def pb_copy(k, source):
        return remote(
            pb.at[z],
            pb.at[source],
            pb_s.at[k],
            pb_r.at[k],
            (lax.rem(z + k, N), tm, hh),
        )

    each(lambda k: pb_copy(k, z).start())

    lane = iota((256, 128), 1)
    row = iota((256, 128), 0)
    many = jnp.where((lane & 15) == (row >> 4), jnp.concatenate([latent] * 16, axis=0), 0.0)
    lane = iota((8, 128), 1)
    row = iota((8, 128), 0)
    pick = ((lane >> 6) == (row >> 1)) & (((lane >> 4) & 3) == (row & 1) + 1)
    pick = jnp.where(pick, 1.0, 0.0)
    lines = lax.dot_general(
        pick, many, NT, preferred_element_type=F32, precision=lax.Precision.HIGHEST
    )
    lat_ref[...] = lines[:4]

    folded_bias = jnp.concatenate(
        [wf[6 + lane_tile // 8, lane_tile % 8][0:1] for lane_tile in range(6)], axis=1
    ) + qb_ref[...].astype(F32)
    cosine = jnp.concatenate([trig[0]] * 8, axis=0)
    sine = jnp.concatenate([trig[1]] * 8, axis=0)
    odd = (iota((128, 128), 1) & 1) == 1

    each(lambda k: pb_copy(k, lax.rem(z + N - k, N)).wait_recv())

    projected = jnp.dot(pb[...].reshape(128, 128), wcc[...], preferred_element_type=F32)
    projected = projected + folded_bias

    def turned(value, gain):
        mean_square = jnp.mean(value * value, axis=1, keepdims=True)
        value = value * lax.rsqrt(mean_square + norm_eps) * gain
        swapped = jnp.where(odd, pltpu.roll(value, 1, 1), pltpu.roll(value, 127, 1))
        return (value * cosine + swapped * sine).astype(BF16)

    q_gain = qg_ref[...].astype(F32)
    k_gain = kg_ref[...].astype(F32)
    for head in range(2):
        at = slice(HD * head, HD * head + HD)
        base = 3 * HD * head
        q_ref[:, at] = turned(projected[:, base : base + HD], q_gain)
        k_ref[:, at] = turned(projected[:, base + HD : base + 2 * HD], k_gain)
        v_ref[:, at] = projected[:, base + 2 * HD : base + 3 * HD].astype(BF16)

    for step in range(1, 5):
        for part in range(4):
            z_right(step, part).wait_send()
            if step < 4:
                z_left(step, part).wait_send()
        y_right(step).wait_send()
        if step < 4:
            y_left(step).wait_send()
    for i in range(5):
        pl.when(halos[i][3])(lambda i=i: halo_copy(i).wait_send())
        pl.when(halos[i][3])(lambda i=i: rh_copy(i).wait_send())
    for k in range(1, 4):
        x_copy(k).wait_send()
    for slot in range(N):
        core_copy(slot).wait_send()
        if slot:
            rz_copy(slot).wait_send()

    def sent(k):
        fold_1(k).wait_send()
        fold_2(k).wait_send()
        fold_3(k, hh).wait_send()
        fold_4(k, tm).wait_send()
        stat_1(k).wait_send()
        stat_2(k).wait_send()
        pb_copy(k, z).wait_send()

    each(sent)


def shards(
    clip_inputs,
    conv_in_weight,
    group_gain,
    group_bias,
    conv_out_weight,
    out_bias,
    patch_weight,
    patch_bias,
    qkv_weight,
    qkv_bias,
    q_gain,
    k_gain,
    frame_pos,
    row_pos,
):
    vmem = pl.BlockSpec(memory_space=pltpu.VMEM)
    smem = pl.BlockSpec(memory_space=pltpu.SMEM)
    dma = pltpu.SemaphoreType.DMA
    latents, queries, keys, values = pl.pallas_call(
        kernel,
        out_shape=(
            jax.ShapeDtypeStruct((4, 256), F32),
            jax.ShapeDtypeStruct((128, 256), BF16),
            jax.ShapeDtypeStruct((128, 256), BF16),
            jax.ShapeDtypeStruct((128, 256), BF16),
        ),
        in_specs=[vmem] * 12 + [smem] * 2,
        out_specs=(vmem,) * 4,
        scratch_shapes=[
            pltpu.VMEM((N, 4, 4, 16, 512), BF16),
            pltpu.VMEM((N, 2, 4, 64, 256), BF16),
            pltpu.VMEM((9, 192, 512), BF16),
            pltpu.VMEM((4, 64, 128), F32),
            pltpu.VMEM((144, 192), BF16),
            pltpu.VMEM((128, 512), BF16),
            pltpu.VMEM((64, 8, 128), F32),
            pltpu.VMEM((N, 8, 8, 128), F32),
            pltpu.VMEM((8, 8, 128), F32),
            pltpu.VMEM((N, 8, 128), F32),
            pltpu.VMEM((N, 8, 128), F32),
            pltpu.VMEM((N, 8, 8, 128), F32),
            pltpu.VMEM((128, 768), BF16),
            pltpu.VMEM((2, 8, 128), F32),
            pltpu.VMEM((N, 8, 128), F32),
            pltpu.VMEM((N, 8, 128), F32),
            pltpu.VMEM((N, 16, 256), F32),
            pltpu.VMEM((N, 16, 256), F32),
            pltpu.VMEM((2, 16, 128), F32),
            pltpu.VMEM((5, 16, 128), F32),
            pltpu.VMEM((N, 16, 128), BF16),
            pltpu.VMEM((2, 16, 128), F32),
            dma((4, 4)),
            dma((4, 4)),
            dma((3, 4)),
            dma((3, 4)),
            dma((5,)),
            dma((5,)),
            dma((4,)),
            dma((4,)),
            dma((4,)),
            dma((4,)),
            dma((3,)),
            dma((3,)),
            dma((N,)),
            dma((N,)),
            dma((4, N)),
            dma((4, N)),
            dma((2, N)),
            dma((2, N)),
            dma((N,)),
            dma((N,)),
            dma((5,)),
            dma((5,)),
            dma((N,)),
            dma((N,)),
        ],
        compiler_params=pltpu.CompilerParams(
            collective_id=0, has_side_effects=True, vmem_limit_bytes=48 * 2**20
        ),
    )(
        clip_inputs[0],
        conv_in_weight,
        group_gain[None],
        group_bias[None],
        conv_out_weight,
        out_bias[None],
        patch_weight,
        patch_bias[None],
        qkv_weight,
        qkv_bias[None],
        q_gain[None],
        k_gain[None],
        frame_pos,
        row_pos,
    )
    merged = (N, 2, 1, 8, 2 * HD)
    return (
        latents.reshape(1, 2, 2, 256),
        queries.reshape(merged),
        keys.reshape(merged),
        values.reshape(merged),
    )


def solution(mesh):
    placed = (
        P("dp", "tm", "height", None, None),
        P(("tm", "height"), "dp"),
        P("dp"),
        P("dp"),
        P(None, "dp", None),
        P(),
        P(),
        P(),
        P(("tm", "height"), "dp"),
        P("dp"),
        P(),
        P(),
        P("tm"),
        P("height"),
    )
    return jax.shard_map(
        shards,
        mesh=mesh,
        in_specs=placed,
        out_specs=(
            P("dp", "tm", "height", None),
            P(None, "tm", "height", None, "dp"),
            P(None, "tm", "height", None, "dp"),
            P(None, "tm", "height", None, "dp"),
        ),
        check_vma=False,
    )
```

time: 752 us -> 91.4 us (0.12)
  waiting for transfers between devices: 449 us -> 0 us
  blocking collectives: 198 us -> 0 us
  Pallas kernels: 0 us -> 83.6 us
  local copies, waits for them, and re-layouts: 47.1 us -> 6.03 us
  matrix products: 15.3 us -> 0 us
  starting transfers between devices: 14.3 us -> 0 us
  between operations: 15.2 us -> 1.49 us
    all_gather x3 -> x0, waiting for transfers between devices: 381 us -> none  [the longest x1 175 us: shards(): lax.all_gather(qkv_weight, ('tm', 'height'), axis=0, tiled=True)]
    psum x1 -> x0, blocking collectives: 179 us -> none  [shards(): lax.psum((sums_local, squares_local), ('tm', 'height'))]
    pallas_call x0 -> x1, Pallas kernels: none -> 83.6 us  [shards(): pl.pallas_call(kernel, out_shape=(jax.ShapeDtypeStruct((4, 256), F32), ja...]
    reduce_scatter x1 -> x0, waiting for transfers between devices: 35.3 us -> none  [shards(): lax.psum_scatter(partial_latent, 'dp', scatter_dimension=0, tiled=True)]
    ppermute x6 -> x0, waiting for transfers between devices: 31.7 us -> none  [the longest x2 19.9 us: padded_2(): lax.ppermute(lax.slice_in_dim(block, 0, width, axis=dim), axis, backward)]
    slice x7 -> x0, local copies, waits for them, and re-layouts: 19.9 us -> none  [the longest x4 19.8 us: convolve(): padded[:, shift_t:shift_t + frames, shift_r:shift_r + rows, shift_c:shift...]
    all_gather x1 -> x0, blocking collectives: 18.5 us -> none  [shards(): lax.all_gather(own_latent.astype(jnp.bfloat16), 'dp', axis=0, tiled=True)]
    dot_general x55 -> x0, matrix products: 15.3 us -> none  [the longest x54 11.9 us: convolve(): jnp.dot(window, weight[9 * shift_t + 3 * shift_r + shift_c], preferred_el...]
  transfers between devices with their start and end apart: 10 -> 0, of which waited for: 10 -> 0; matrix products, arithmetic and copies ran while one was open for 2% -> 0% of each run, Pallas kernels for 0% -> 0%
where the time goes in v1:
time: 91.4 us; the launch traced here: 91.1 us
  Pallas kernels  83.6 us (91%)
  local copies, waits for them, and re-layouts  6.03 us (7%)
  between operations  1.49 us (2%)
    pallas_call x1, Pallas kernels, shards(): pl.pallas_call(kernel, out_shape=(jax.ShapeDtypeStruct((4, 256), F32), ja...  83.6 us
    unnamed x23, local copies, waits for them, and re-layouts  4.04 us

profile of v1, /device:TPU:1, one launch (start us, length us, event | category | flops | bytes accessed | tf_op | source)
XLA Modules:
  0.0 91.1 jit_solution(16109976100995476447)
XLA Ops:
  0.6 0.0 copy-start
  1.3 0.7 broadcast_in_dim.25.qb_ref
  2.0 0.7 broadcast_in_dim.24.pb_ref
  2.7 0.9 copy.18.wi_ref
  3.6 0.0 copy-start.1
  3.6 0.0 copy-start.2
  3.6 0.0 copy-start.3
  3.6 0.0 copy-start.4
  3.6 0.0 copy-start.5
  3.7 0.0 copy-start.6
  3.7 0.0 copy-start.7
  3.7 0.0 copy-start.8
  3.7 1.2 %copy.19.wo_ref = bf16[27,64,16]{2,1,0:T(8,128)(2,1)S(1)} copy(bf16[27,64,16]{1,2,0:T(8,128)(2,1)} %param.18) | data formatting | bytes 110592 | tf_op args[4]
  4.9 0.0 copy-done
  4.9 0.0 copy-done.1
  5.0 0.0 copy-done.2
  5.0 0.0 copy-done.3
  5.0 0.0 copy-done.4
  5.0 0.0 copy-done.5
  5.0 0.0 copy-done.6
  5.0 0.0 copy-done.7
  5.0 0.0 copy-done.8
  5.0 83.6 %shard_map.165 = (f32[4,256]{1,0:T(4,128)S(1)}, bf16[128,256]{1,0:T(8,128)(2,1)S(1)}, bf16[128,256]{1,0:T(8,128)(2,1)S(1)}, bf16[128,256]{1,0:T(8,128)(2,1)S(1)}) custom-call(bf16[2,2,16,512]{3,2,1,0:T(8,128)(2,1)S(1)} %bitcast.18, bf16[216,64]{1,0:T(8,128)(2,1)S(1)} %copy.18.wi_ref, bf16[1,64]{1,0:T(2,128)(2,1)S(1)} %bitcast.19, ...), custom_call_target="tpu_custom_call" | custom-call | tf_op jit(solution)/shard_map/pallas_call | solution.py:763
  88.6 0.6 reshape.20
  89.2 0.6 copy.27
  89.8 0.6 copy.28
  90.4 0.6 copy.29
Async XLA Ops:
  0.6 4.3 %copy-start = (bf16[64,3072]{1,0:T(8,128)(2,1)S(1)}, bf16[64,3072]{1,0:T(8,128)(2,1)}, u32[]{:S(2)}) copy-start(bf16[64,3072]{1,0:T(8,128)(2,1)} %pw_ref.1) | copy-start | bytes 1179652
  3.6 1.4 %copy-start.1 = (bf16[48,768]{1,0:T(8,128)(2,1)S(1)}, bf16[48,768]{1,0:T(8,128)(2,1)}, u32[]{:S(2)}) copy-start(bf16[48,768]{1,0:T(8,128)(2,1)} %qw_ref.1) | copy-start | bytes 221188
  3.6 1.3 %copy-start.2 = (bf16[1,2,2,16,512]{4,3,2,1,0:T(8,128)(2,1)S(1)}, bf16[1,2,2,16,512]{4,3,2,1,0:T(8,128)(2,1)}, u32[]{:S(2)}) copy-start(bf16[1,2,2,16,512]{4,3,2,1,0:T(8,128)(2,1)} %param.14) | copy-start | bytes 196612
  3.6 1.3 %copy-start.3 = (bf16[64]{0:T(256)(128)(2,1)S(1)}, bf16[64]{0:T(256)(128)(2,1)}, u32[]{:S(2)}) copy-start(bf16[64]{0:T(256)(128)(2,1)} %param.16) | copy-start | bytes 388
  3.6 1.3 %copy-start.4 = (bf16[64]{0:T(256)(128)(2,1)S(1)}, bf16[64]{0:T(256)(128)(2,1)}, u32[]{:S(2)}) copy-start(bf16[64]{0:T(256)(128)(2,1)} %param.17) | copy-start | bytes 388
  3.6 1.3 %copy-start.5 = (f32[16]{0:T(128)S(1)}, f32[16]{0:T(128)}, u32[]{:S(2)}) copy-start(f32[16]{0:T(128)} %param.19) | copy-start | bytes 196
  3.7 1.3 %copy-start.6 = (bf16[128]{0:T(256)(128)(2,1)S(1)}, bf16[128]{0:T(256)(128)(2,1)}, u32[]{:S(2)}) copy-start(bf16[128]{0:T(256)(128)(2,1)} %param.24) | copy-start | bytes 772
  3.7 1.3 %copy-start.7 = (bf16[128]{0:T(256)(128)(2,1)S(1)}, bf16[128]{0:T(256)(128)(2,1)}, u32[]{:S(2)}) copy-start(bf16[128]{0:T(256)(128)(2,1)} %param.25) | copy-start | bytes 772
  3.7 1.3 %copy-start.8 = (s32[2]{0:T(128)S(1)}, s32[2]{0:T(128)}, u32[]{:S(2)}) copy-start(s32[2]{0:T(128)} %fp_ref.1) | copy-start | bytes 28

commit v2 on v1

v2 whole, which is shorter than its diff:
```python
import math

import jax
import jax.numpy as jnp
from jax import lax
from jax.experimental import pallas as pl
from jax.experimental.pallas import tpu as pltpu
from jax.sharding import PartitionSpec as P

HD = 128
GROUPS = 32
TAPS = 27
N = 8

norm_eps = 1e-06
latent_scale = 0.476986
rope_base = 256.0
time_dims = 16
row_dims = 56

F32 = jnp.float32
BF16 = jnp.bfloat16
MESH = pl.DeviceIdType.MESH

SLOT_STEP = (0, -1, 1, -2, 2, -3, 3, -4)

ROW = (2, 0, 1, 3)

NT = (((1,), (1,)), ((), ()))


def iota(shape, dim):
    return lax.broadcasted_iota(jnp.int32, shape, dim)


def part_of(ref, which):
    frames, rows = ((2, 0), (0, 0), (2, 2), (0, 2))[which]
    return ref.at[pl.ds(frames, 2), pl.ds(rows, 2)]


def kernel(
    x_ref,
    wi_ref,
    gg_ref,
    gb_ref,
    wo_ref,
    ob_ref,
    pw_ref,
    pb_ref,
    qw_ref,
    qb_ref,
    qg_ref,
    kg_ref,
    fp_ref,
    rp_ref,
    lat_ref,
    pat_ref,
    wcc_ref,
    bias_ref,
    trig_ref,
    xe,
    wi,
    gg,
    gb,
    wo,
    ob,
    pw,
    pbias,
    qw,
    qb,
    qg,
    kg,
    wg,
    bt,
    ht,
    w2,
    place,
    wp,
    wr,
    wsum,
    wrh,
    wth,
    wf,
    st,
    outs,
    rz,
    ext,
    rh,
    pb,
    in_sem,
    zr_s,
    zr_r,
    zl_s,
    zl_r,
    ha_s,
    ha_r,
    cc_s,
    cc_r,
    wy_s,
    wy_r,
    wx_s,
    wx_r,
    co_s,
    co_r,
    wc_s,
    wc_r,
    ss_s,
    ss_r,
    rz_s,
    rz_r,
    rh_s,
    rh_r,
    pb_s,
    pb_r,
):
    z = lax.axis_index("dp")
    tm = lax.axis_index("tm")
    hh = lax.axis_index("height")
    core = lax.rem(tm, 2)
    y_lo = tm // 2
    x = hh // 2
    y_hi = lax.rem(hh, 2)
    y = y_hi * 4 + y_lo

    def at_y(where):
        return (z, lax.rem(where, 4) * 2 + core, x * 2 + where // 4)

    def remote(src, dst, send, recv, device):
        return pltpu.make_async_remote_copy(
            src_ref=src,
            dst_ref=dst,
            send_sem=send,
            recv_sem=recv,
            device_id=device,
            device_id_type=MESH,
        )

    sent = []

    def go(copy):
        copy.start()
        sent.append(copy.wait_send)

    def go_if(condition, make):
        pl.when(condition)(lambda: make().start())
        sent.append(lambda: pl.when(condition)(lambda: make().wait_send()))

    def each(fn, end=N):
        def body(k, _):
            fn(k)
            return 0

        lax.fori_loop(1, end, body, 0)

    def go_each(make, end=N):
        each(lambda k: make(k).start(), end)
        sent.append(lambda: each(lambda k: make(k).wait_send(), end))

    def finish():
        for wait in sent:
            wait()

    z_up = (lax.rem(z + 1, N), tm, hh)
    z_down = (lax.rem(z + N - 1, N), tm, hh)
    other_core = (z, tm + 1 - 2 * core, hh)
    first_core = core == 0
    last_core = core == 1

    barrier = pltpu.get_barrier_semaphore()

    def greet(device):
        pl.semaphore_signal(barrier, inc=1, device_id=device, device_id_type=MESH)

    def in_plane(k):
        return (z, lax.rem(tm + k // N, N), lax.rem(hh + lax.rem(k, N), N))

    each(lambda k: greet((lax.rem(z + k, N), tm, hh)))
    each(lambda k: greet(in_plane(k)), N * N)

    d = tm * N + hh
    tile = jnp.minimum(48 * d // 128, 22)
    shift = 48 * d - 128 * tile
    window = pl.ds(pl.multiple_of(tile * 128, 128), 256)
    own = xe.at[0]
    staged = [
        (wi_ref, wi),
        (x_ref, part_of(own, 0)),
        (pw_ref.at[:, window], pw),
        (pb_ref, pbias),
        (qw_ref, qw),
        (wo_ref, wo),
        (gg_ref, gg),
        (gb_ref, gb),
        (ob_ref, ob),
        (qb_ref, qb),
        (qg_ref, qg),
        (kg_ref, kg),
    ]
    staged = [
        pltpu.make_async_copy(src, dst, in_sem.at[i]) for i, (src, dst) in enumerate(staged)
    ]
    for copy in staged:
        copy.start()

    wg[y, core, x] = jnp.zeros((64, 256), BF16)
    staged[0].wait()
    wg[y, core, x, :, pl.ds(0, 216)] = wi[...]
    staged[1].wait()

    pl.semaphore_wait(barrier, N - 1 + N * N - 1)

    def z_right(step, part):
        return remote(
            part_of(xe.at[SLOT_STEP.index(1 - step)], part),
            part_of(xe.at[SLOT_STEP.index(-step)], part),
            zr_s.at[step - 1, part],
            zr_r.at[step - 1, part],
            z_up,
        )

    def z_left(step, part):
        return remote(
            part_of(xe.at[SLOT_STEP.index(step - 1)], part),
            part_of(xe.at[SLOT_STEP.index(step)], part),
            zl_s.at[step - 1, part],
            zl_r.at[step - 1, part],
            z_down,
        )

    def z_first(part):
        if part in (0, 2):
            go(z_right(1, part))
            go(z_left(1, part))
        else:
            go_if(first_core, lambda: z_right(1, part))
            go_if(first_core, lambda: z_left(1, part))

    has_next = tm < N - 1
    has_last = tm > 0
    has_up = hh < N - 1
    has_down = hh > 0
    next_tm = lax.rem(tm + 1, N)
    up_h = lax.rem(hh + 1, N)
    down_h = lax.rem(hh + N - 1, N)
    row_0 = own.at[pl.ds(2, 2), pl.ds(0, 1)]
    row_1 = own.at[pl.ds(2, 2), pl.ds(1, 1)]
    halos = (
        (part_of(own, 0), part_of(own, 1), (z, next_tm, hh), has_next, has_last),
        (row_0, own.at[pl.ds(2, 2), pl.ds(3, 1)], (z, tm, down_h), has_down, has_up),
        (row_1, own.at[pl.ds(2, 2), pl.ds(2, 1)], (z, tm, up_h), has_up, has_down),
        (
            row_0,
            own.at[pl.ds(0, 2), pl.ds(3, 1)],
            (z, next_tm, down_h),
            last_core & has_next & has_down,
            first_core & has_last & has_up,
        ),
        (
            row_1,
            own.at[pl.ds(0, 2), pl.ds(2, 1)],
            (z, next_tm, up_h),
            last_core & has_next & has_up,
            first_core & has_last & has_down,
        ),
    )

    def halo_copy(i):
        src, dst, device, _, _ = halos[i]
        return remote(src, dst, ha_s.at[i], ha_r.at[i], device)

    def halo_wait(i):
        pl.when(halos[i][4])(lambda: halo_copy(i).wait_recv())

    for i in (3, 4, 1, 2, 0):
        go_if(halos[i][3], lambda i=i: halo_copy(i))
    z_first(0)

    def y_copy(k, source):
        return remote(
            wg.at[y, core, x],
            wg.at[source, core, x],
            wy_s.at[k],
            wy_r.at[k],
            at_y(lax.rem(y + k, N)),
        )

    def x_copy(k, i, source):
        line = lax.rem(y + N - k, N)
        return remote(
            wg.at[line, core, x],
            wg.at[line, core, source],
            wx_s.at[k, i],
            wx_r.at[k, i],
            (z, tm, lax.rem(hh + 2 * i, N)),
        )

    def core_copy(k, source):
        line = lax.rem(y + N - k, N)
        return remote(
            wg.at[line, core], wg.at[line, source], co_s.at[k], co_r.at[k], other_core
        )

    y_order = (1, 7, 2, 6, 3, 5, 4)
    for k in y_order:
        go(y_copy(k, y))
    for i in (1, 3, 2):
        go(x_copy(0, i, x))

    for copy in staged[2:5]:
        copy.wait()
    bias_rows = pbias[...].astype(F32)
    bias_tile = iota((24, 128), 0)
    bias_row = jnp.concatenate(
        [
            jnp.sum(jnp.where(bias_tile == tile + i, bias_rows, 0.0), axis=0, keepdims=True)
            for i in range(2)
        ],
        axis=1,
    )
    embed = jnp.concatenate([pw[...].astype(F32), jnp.broadcast_to(bias_row, (8, 256))], axis=0)
    embed = pltpu.roll(embed, lax.rem(256 - shift, 256), 1)[:, :48].astype(BF16)
    part = jnp.dot(embed, qw[...], preferred_element_type=F32)
    for row in range(9):
        for lane in range(6):
            wp[row * 6 + lane] = part[8 * row : 8 * row + 8, 128 * lane : 128 * lane + 128]
    wp[pl.ds(54, 10)] = jnp.zeros((10, 8, 128), F32)

    def fold_1(k):
        to = lax.rem(tm + k, N)
        return remote(
            wp.at[pl.ds(8 * to, 8)], wr.at[k], wc_s.at[0, k], wc_r.at[0, k], (z, to, hh)
        )

    def fold_2(k):
        to = lax.rem(hh + k, N)
        return remote(wsum.at[to], wrh.at[k], wc_s.at[1, k], wc_r.at[1, k], (z, tm, to))

    def fold_3(k, source):
        to = lax.rem(hh + k, N)
        return remote(
            wth.at[hh], wth.at[source], wc_s.at[2, k], wc_r.at[2, k], (z, tm, to)
        )

    def fold_4(k, source):
        to = lax.rem(tm + k, N)
        return remote(
            wf.at[tm], wf.at[source], wc_s.at[3, k], wc_r.at[3, k], (z, to, hh)
        )

    go_each(lambda k: fold_1(k))

    def to_core(slot, part):
        return remote(
            part_of(xe.at[slot], part),
            part_of(xe.at[slot], part + 1),
            cc_s.at[slot, part // 2],
            cc_r.at[slot, part // 2],
            other_core,
        )

    def ring_part(step, part):
        def pass_on():
            z_right(step, part).wait_recv()
            if step < 4:
                z_right(step + 1, part).start()
                z_left(step, part).wait_recv()
            if step < 3:
                z_left(step + 1, part).start()

        def passed():
            if step < 4:
                z_right(step + 1, part).wait_send()
            if step < 3:
                z_left(step + 1, part).wait_send()

        if part in (1, 3):
            pl.when(first_core)(pass_on)
            sent.append(lambda: pl.when(first_core)(passed))
            return
        pass_on()
        sent.append(passed)
        go_if(first_core, lambda: to_core(2 * step - 1, part))
        if step < 4:
            go_if(first_core, lambda: to_core(2 * step, part))

    def core_arrived(slot):
        @pl.when(last_core)
        def _():
            if slot:
                to_core(slot, 0).wait_recv()
            to_core(slot, 2).wait_recv()

    halo_wait(0)

    @pl.when(jnp.logical_not(has_last))
    def _():
        first = xe[0, 2:3, 0:2]
        xe[0, 0:1, 0:2] = first
        xe[0, 1:2, 0:2] = first

    z_first(1)
    ring_part(1, 0)
    ring_part(1, 1)
    halo_wait(1)
    halo_wait(2)

    @pl.when(jnp.logical_not(has_down))
    def _():
        xe[0, 2:4, 2:3] = xe[0, 2:4, 0:1]

    @pl.when(jnp.logical_not(has_up))
    def _():
        xe[0, 2:4, 3:4] = xe[0, 2:4, 1:2]

    z_first(2)
    go_if(first_core, lambda: to_core(0, 2))
    halo_wait(3)
    halo_wait(4)

    @pl.when(jnp.logical_not(has_last))
    def _():
        first = xe[0, 2:3, 2:4]
        xe[0, 0:1, 2:4] = first
        xe[0, 1:2, 2:4] = first

    @pl.when(first_core & has_last & jnp.logical_not(has_down))
    def _():
        xe[0, 0:2, 2:3] = xe[0, 0:2, 0:1]

    @pl.when(first_core & has_last & jnp.logical_not(has_up))
    def _():
        xe[0, 0:2, 3:4] = xe[0, 0:2, 1:2]

    z_first(3)

    ring_part(2, 0)
    for k in y_order:
        y_copy(k, lax.rem(y + N - k, N)).wait_recv()
        for i in (1, 3, 2):
            go(x_copy(k, i, x))

    ring_part(2, 1)
    for part in (2, 3):
        ring_part(1, part)
    ring_part(3, 0)
    ring_part(3, 1)
    for part in (2, 3):
        ring_part(2, part)

    staged[5].wait()
    for ij in range(9):
        w2[16 * ij : 16 * ij + 16] = jnp.concatenate(
            [wo[3 * ij + l].astype(F32) for l in range(3)], axis=1
        ).astype(BF16)

    lane = iota((128, 512), 1)
    row = iota((128, 512), 0)
    s_at = (lane >> 6) & 3
    q_at = (lane >> 4) & 3
    f_at = (row >> 5) & 1
    r_at = (row >> 4) & 1
    in_frame = (s_at == f_at + 2) | ((tm == 0) & (s_at < 2) & (f_at == 0))
    in_row = (
        (q_at == r_at + 1)
        | ((hh == 0) & (q_at == 0) & (r_at == 0))
        | ((hh == N - 1) & (q_at == 3) & (r_at == 1))
    )
    same = ((lane & 15) == (row & 15)) & ((lane >> 8) == (row >> 6))
    place[...] = jnp.where(in_frame & in_row & same, 1.0, 0.0).astype(BF16)

    for copy in staged[6:]:
        copy.wait()
    entry = iota((16, 128), 1) >> 1
    token = iota((16, 128), 0)
    is_frame = entry < 8
    is_row = entry < 36
    start = jnp.where(is_frame, 0, jnp.where(is_row, 8, 36))
    width = jnp.where(is_frame, float(time_dims), float(row_dims))
    power = 2.0 * (entry - start).astype(F32) / width
    freq = jnp.exp(power * (-math.log(rope_base)))
    frame_at = jnp.where(token < 8, fp_ref[0].astype(F32), fp_ref[1].astype(F32))
    spot = jnp.where(
        is_frame,
        frame_at,
        jnp.where(is_row, rp_ref[0].astype(F32), (token & 7).astype(F32)),
    )
    angle = spot * freq
    odd = (iota((16, 128), 1) & 1) == 1
    cosine = jnp.cos(angle)
    sine = jnp.sin(angle)
    sine = jnp.where(odd, sine, -sine)
    for i, gain_of in enumerate((qg, kg)):
        gain_row = jnp.broadcast_to(gain_of[...].astype(F32), (16, 128))
        swapped = jnp.where(odd, pltpu.roll(gain_row, 1, 1), pltpu.roll(gain_row, 127, 1))
        trig_ref[2 * i] = cosine * gain_row
        trig_ref[2 * i + 1] = sine * swapped

    for k in (0,) + y_order:
        for i in range(1, 4):
            x_copy(k, i, lax.rem(x + 4 - i, 4)).wait_recv()
        go(core_copy(k, core))

    for part in (2, 3):
        ring_part(3, part)

    each(lambda k: fold_1(k).wait_recv())
    total = wp[pl.ds(8 * tm, 8)]
    for k in range(1, N):
        total = total + wr[k]
    wsum[...] = total
    go_each(lambda k: fold_2(k))

    for k in range(N):
        core_copy(k, 1 - core).wait_recv()

    def shard_of(index):
        t, h = index // N, index % N
        return wg[(h % 2) * 4 + t // 2, t % 2, h // 2]

    for tile in range(4 * TAPS):
        source, first = (128 * tile) // 216, (128 * tile) % 216
        count = min(128, 216 - first)
        value = shard_of(source)[:, first : first + count]
        if count < 128:
            value = jnp.concatenate([value, shard_of(source + 1)[:, : 128 - count]], axis=1)
        tap = tile // 4
        ij, l = tap // 3, tap % 3
        at = 128 * (tile % 4)
        bt[ij, 64 * l : 64 * l + 64, at : at + 128] = value

    col = iota((64, 128), 1) & 15

    def conv_pair(pair):
        total = jnp.zeros((192, 128), F32)
        for ij in range(9):
            i, j = ij // 3, ij % 3
            rows = [xe[2 * pair : 2 * pair + 2, i : i + 2, ROW[j + r]] for r in range(2)]
            block = jnp.stack(rows, axis=2).reshape(128, 512)
            total = total + lax.dot_general(bt[ij], block, NT, preferred_element_type=F32)
        left, mid, right = total[:64], total[64:128], total[128:]
        left = jnp.where(col == 0, left, pltpu.roll(left, 1, 1))
        right = jnp.where(col == 15, right, pltpu.roll(right, 127, 1))
        ht[pair] = left + mid + right

    for pair in range(3):
        core_arrived(2 * pair)
        core_arrived(2 * pair + 1)
        conv_pair(pair)
    for part in range(4):
        ring_part(4, part)
    core_arrived(6)
    core_arrived(7)
    conv_pair(3)

    stat_lane = iota((8, 128), 1)
    compact = jnp.zeros((8, 128), F32)
    for pair in range(4):
        value = ht[pair]
        sums = jnp.sum(value.reshape(4, 16, 128), axis=1)
        squares = jnp.sum((value * value).reshape(4, 16, 128), axis=1)
        both = jnp.concatenate([sums, squares], axis=0)
        low = jnp.sum(jnp.where(stat_lane < 64, both, 0.0), axis=1, keepdims=True)
        high = jnp.sum(jnp.where(stat_lane >= 64, both, 0.0), axis=1, keepdims=True)
        compact = jnp.where(stat_lane == pair, low, compact)
        compact = jnp.where(stat_lane == 64 + pair, high, compact)
    st[0, 0:1] = jnp.sum(pltpu.roll(compact, 0, 1, stride=4, stride_axis=0), axis=0, keepdims=True)

    def stat_copy(k):
        return remote(
            st.at[0, pl.ds(0, 1)], st.at[k, pl.ds(0, 1)], ss_s.at[k], ss_r.at[k], in_plane(k)
        )

    go_each(stat_copy, N * N)

    each(lambda k: fold_2(k).wait_recv())
    tile_sum = wsum[hh]
    for k in range(1, N):
        tile_sum = tile_sum + wrh[k]
    wth[hh] = tile_sum
    go_each(lambda k: fold_3(k, hh))

    diag = iota((64, 64), 0) == iota((64, 64), 1)
    gain = jnp.sum(jnp.where(diag, gg[...].astype(F32), 0.0), axis=1, keepdims=True)
    bias = jnp.sum(jnp.where(diag, gb[...].astype(F32), 0.0), axis=1, keepdims=True)
    diag = iota((16, 16), 0) == iota((16, 16), 1)
    out_bias = jnp.sum(jnp.where(diag, ob[...], 0.0), axis=1, keepdims=True)

    each(lambda k: stat_copy(k).wait_recv(), N * N)
    total = jnp.zeros((1, 128), F32)
    for k in range(N * N):
        total = total + st[k, 0:1]
    total = jnp.broadcast_to(total, (8, 128))
    compact = pltpu.roll(total, 100, 1, stride=4, stride_axis=0)
    count = float(16 * 16 * 16 * 16)
    average = compact / count
    mean = average
    var = pltpu.roll(average, 4, 0) - mean * mean
    inv = lax.rsqrt(var + norm_eps)

    wide = iota((16, 512), 1)
    t_at = (wide >> 6) & 3
    u_at = (wide >> 4) & 3
    lane_128 = iota((8, 128), 1)

    def spread(value, pair):
        lanes = jnp.where(
            lane_128 < 64,
            jnp.broadcast_to(value[:, pair : pair + 1], (8, 128)),
            jnp.broadcast_to(value[:, 64 + pair : 65 + pair], (8, 128)),
        )
        return jnp.concatenate(
            [jnp.broadcast_to(lanes[7 - g : 8 - g], (16, 128)) for g in range(4)], axis=0
        )

    def rz_copy(slot):
        to = lax.rem(z + N + SLOT_STEP[slot], N)
        return remote(outs.at[slot], rz.at[slot], rz_s.at[slot], rz_r.at[slot], (to, tm, hh))

    for pair in (3, 2, 1, 0):
        scale = spread(inv, pair) * gain
        offset = bias - spread(mean, pair) * scale
        value = ht[pair] * scale + offset
        value = value / (1.0 + jnp.exp(-value))
        left = jnp.where(col == 0, value, pltpu.roll(value, 1, 1))
        right = jnp.where(col == 15, value, pltpu.roll(value, 127, 1))
        stacked = jnp.concatenate([left, value, right], axis=0).astype(BF16)
        spots = jnp.dot(stacked, place[...], preferred_element_type=F32).astype(BF16)
        taps = jnp.dot(w2[...], spots, preferred_element_type=F32)
        total = jnp.zeros((16, 512), F32)
        for ij in range(9):
            i, j = ij // 3, ij % 3
            move = (16 * (1 - j) - 64 * i) % 512
            moved = taps[16 * ij : 16 * ij + 16]
            if move:
                moved = pltpu.roll(moved, move, 1)
            valid = t_at <= 3 - i
            if j == 0:
                valid = valid & (u_at >= 1)
            if j == 2:
                valid = valid & (u_at <= 2)
            total = total + jnp.where(valid, moved, 0.0)
        outs[2 * pair] = total[:, :256]
        outs[2 * pair + 1] = total[:, 256:]
        for slot in (2 * pair + 1, 2 * pair):
            if slot:
                go(rz_copy(slot))

    goes = (
        has_next,
        has_down,
        has_up,
        has_next & has_down,
        has_next & has_up,
    )
    comes = (
        has_last,
        has_up,
        has_down,
        has_last & has_up,
        has_last & has_down,
    )
    for i in range(5):

        @pl.when(jnp.logical_not(comes[i]))
        def _(i=i):
            rh[i] = jnp.zeros((16, 128), F32)

    each(lambda k: fold_3(k, lax.rem(hh + N - k, N)).wait_recv())
    wf[tm] = wth[...]
    go_each(lambda k: fold_4(k, tm))

    total = outs[0]
    for slot in range(1, N):
        rz_copy(slot).wait_recv()
        total = total + rz[slot]
    ext[0] = total[:, :128]
    ext[1] = total[:, 128:]

    def rh_copy(i):
        return remote(
            ext.at[1 if i in (0, 3, 4) else 0],
            rh.at[i],
            rh_s.at[i],
            rh_r.at[i],
            halos[i][2],
        )

    for i in range(5):
        go_if(goes[i], lambda i=i: rh_copy(i))
    for i in range(5):
        pl.when(comes[i])(lambda i=i: rh_copy(i).wait_recv())

    narrow = iota((16, 128), 1)
    u_at = (narrow >> 4) & 3
    inside = (u_at == 1) | (u_at == 2)
    latent = jnp.where(inside, total[:, :128] + rh[0], 0.0)
    latent = latent + jnp.where(u_at == 2, pltpu.roll(rh[1] + rh[3], 32, 1), 0.0)
    latent = latent + jnp.where(u_at == 1, pltpu.roll(rh[2] + rh[4], 96, 1), 0.0)
    latent = (latent + out_bias) * latent_scale

    lane = iota((128, 128), 1)
    group = (iota((128, 128), 0) >> 4) & 3
    keep = (((lane >> 4) & 3) == (group >> 1) + 1) & ((lane & 1) == (group & 1))
    rounded = latent.astype(BF16).astype(F32)
    many = jnp.where(keep, jnp.concatenate([rounded] * 8, axis=0), 0.0).astype(BF16)
    lane = iota((16, 128), 1)
    row = iota((16, 128), 0)
    pick = ((lane >> 6) == (row >> 3)) & (((lane & 15) >> 1) == (row & 7))
    pick = jnp.where(pick, 1.0, 0.0).astype(BF16)
    pb[z] = lax.dot_general(pick, many, NT, preferred_element_type=F32).astype(BF16)

    def pb_copy(k, source):
        return remote(
            pb.at[z],
            pb.at[source],
            pb_s.at[k],
            pb_r.at[k],
            (lax.rem(z + k, N), tm, hh),
        )

    go_each(lambda k: pb_copy(k, z))

    each(lambda k: fold_4(k, lax.rem(tm + N - k, N)).wait_recv())
    for lane_tile in range(6):
        for pair in range(4):
            tiles = [12 * pair + lane_tile, 12 * pair + 6 + lane_tile]
            value = jnp.concatenate([wf[t // 8, t % 8] for t in tiles], axis=0)
            high = value.astype(BF16)
            low = (value - high.astype(F32)).astype(BF16)
            at = slice(128 * lane_tile, 128 * lane_tile + 128)
            wcc_ref[16 * pair : 16 * pair + 16, at] = high
            wcc_ref[64 + 16 * pair : 64 + 16 * pair + 16, at] = low
    proj_bias = qb[...].astype(F32)
    bias_ref[...] = jnp.concatenate(
        [
            wf[6 + lane_tile // 8, lane_tile % 8][0:1] + proj_bias[lane_tile : lane_tile + 1]
            for lane_tile in range(6)
        ],
        axis=1,
    )

    lane = iota((256, 128), 1)
    row = iota((256, 128), 0)
    many = jnp.where((lane & 15) == (row >> 4), jnp.concatenate([latent] * 16, axis=0), 0.0)
    lane = iota((8, 128), 1)
    row = iota((8, 128), 0)
    pick = ((lane >> 6) == (row >> 1)) & (((lane >> 4) & 3) == (row & 1) + 1)
    pick = jnp.where(pick, 1.0, 0.0)
    lines = lax.dot_general(
        pick, many, NT, preferred_element_type=F32, precision=lax.Precision.HIGHEST
    )
    lat_ref[...] = lines[:4]

    each(lambda k: pb_copy(k, lax.rem(z + N - k, N)).wait_recv())
    pat_ref[...] = pb[...].reshape(128, 128)

    finish()


def project(lat_in, pat_ref, wcc_ref, bias_ref, trig_ref, lat_ref, q_ref, k_ref, v_ref):
    for row in range(4):
        lat_ref[0, row // 2, row % 2 : row % 2 + 1] = lat_in[row : row + 1]
    odd = (iota((128, 128), 1) & 1) == 1
    projected = jnp.dot(pat_ref[...], wcc_ref[...], preferred_element_type=F32)
    projected = projected + bias_ref[...]

    def turned(value, which):
        cosine = jnp.concatenate([trig_ref[2 * which]] * 8, axis=0)
        sine = jnp.concatenate([trig_ref[2 * which + 1]] * 8, axis=0)
        mean_square = jnp.mean(value * value, axis=1, keepdims=True)
        value = value * lax.rsqrt(mean_square + norm_eps)
        swapped = jnp.where(odd, pltpu.roll(value, 1, 1), pltpu.roll(value, 127, 1))
        return (value * cosine + swapped * sine).astype(BF16)

    for head in range(2):
        at = slice(HD * head, HD * head + HD)
        base = 3 * HD * head
        q_ref[:, at] = turned(projected[:, base : base + HD], 0)
        k_ref[:, at] = turned(projected[:, base + HD : base + 2 * HD], 1)
        v_ref[:, at] = projected[:, base + 2 * HD : base + 3 * HD].astype(BF16)


def shards(
    clip_inputs,
    conv_in_weight,
    group_gain,
    group_bias,
    conv_out_weight,
    out_bias,
    patch_weight,
    patch_bias,
    qkv_weight,
    qkv_bias,
    q_gain,
    k_gain,
    frame_pos,
    row_pos,
):
    vmem = pl.BlockSpec(memory_space=pltpu.VMEM)
    smem = pl.BlockSpec(memory_space=pltpu.SMEM)
    hbm = pl.BlockSpec(memory_space=pltpu.HBM)
    dma = pltpu.SemaphoreType.DMA
    travelled = pl.pallas_call(
        kernel,
        out_shape=(
            jax.ShapeDtypeStruct((4, 256), F32),
            jax.ShapeDtypeStruct((128, 128), BF16),
            jax.ShapeDtypeStruct((128, 768), BF16),
            jax.ShapeDtypeStruct((1, 768), F32),
            jax.ShapeDtypeStruct((4, 16, 128), F32),
        ),
        in_specs=[hbm] * 12 + [smem] * 2,
        out_specs=(vmem,) * 5,
        scratch_shapes=[
            pltpu.VMEM((N, 4, 4, 16, 512), BF16),
            pltpu.VMEM((64, 216), BF16),
            pltpu.VMEM((1, 64), BF16),
            pltpu.VMEM((1, 64), BF16),
            pltpu.VMEM((TAPS, 16, 64), BF16),
            pltpu.VMEM((1, 16), F32),
            pltpu.VMEM((64, 256), BF16),
            pltpu.VMEM((24, 128), BF16),
            pltpu.VMEM((48, 768), BF16),
            pltpu.VMEM((6, 128), BF16),
            pltpu.VMEM((1, 128), BF16),
            pltpu.VMEM((1, 128), BF16),
            pltpu.VMEM((N, 2, 4, 64, 256), BF16),
            pltpu.VMEM((9, 192, 512), BF16),
            pltpu.VMEM((4, 64, 128), F32),
            pltpu.VMEM((144, 192), BF16),
            pltpu.VMEM((128, 512), BF16),
            pltpu.VMEM((64, 8, 128), F32),
            pltpu.VMEM((N, 8, 8, 128), F32),
            pltpu.VMEM((8, 8, 128), F32),
            pltpu.VMEM((N, 8, 128), F32),
            pltpu.VMEM((N, 8, 128), F32),
            pltpu.VMEM((N, 8, 8, 128), F32),
            pltpu.VMEM((N * N, 8, 128), F32),
            pltpu.VMEM((N, 16, 256), F32),
            pltpu.VMEM((N, 16, 256), F32),
            pltpu.VMEM((2, 16, 128), F32),
            pltpu.VMEM((5, 16, 128), F32),
            pltpu.VMEM((N, 16, 128), BF16),
            dma((12,)),
            dma((4, 4)),
            dma((4, 4)),
            dma((3, 4)),
            dma((3, 4)),
            dma((5,)),
            dma((5,)),
            dma((N, 2)),
            dma((N, 2)),
            dma((N,)),
            dma((N,)),
            dma((N, 4)),
            dma((N, 4)),
            dma((N,)),
            dma((N,)),
            dma((4, N)),
            dma((4, N)),
            dma((N * N,)),
            dma((N * N,)),
            dma((N,)),
            dma((N,)),
            dma((5,)),
            dma((5,)),
            dma((N,)),
            dma((N,)),
        ],
        compiler_params=pltpu.CompilerParams(
            collective_id=0, has_side_effects=True, vmem_limit_bytes=63 * 2**20
        ),
    )(
        clip_inputs[0],
        conv_in_weight.T,
        group_gain[None],
        group_bias[None],
        conv_out_weight.transpose(0, 2, 1),
        out_bias[None],
        patch_weight,
        patch_bias.reshape(24, 128),
        qkv_weight,
        qkv_bias.reshape(6, 128),
        q_gain[None],
        k_gain[None],
        frame_pos,
        row_pos,
    )
    latents, queries, keys, values = pl.pallas_call(
        project,
        out_shape=(
            jax.ShapeDtypeStruct((1, 2, 2, 256), F32),
            jax.ShapeDtypeStruct((128, 256), BF16),
            jax.ShapeDtypeStruct((128, 256), BF16),
            jax.ShapeDtypeStruct((128, 256), BF16),
        ),
        in_specs=[vmem] * 5,
        out_specs=(vmem,) * 4,
    )(*travelled)
    merged = (N, 2, 1, 8, 2 * HD)
    return (
        latents,
        queries.reshape(merged),
        keys.reshape(merged),
        values.reshape(merged),
    )


def solution(mesh):
    placed = (
        P("dp", "tm", "height", None, None),
        P(("tm", "height"), "dp"),
        P("dp"),
        P("dp"),
        P(None, "dp", None),
        P(),
        P(),
        P(),
        P(("tm", "height"), "dp"),
        P("dp"),
        P(),
        P(),
        P("tm"),
        P("height"),
    )
    return jax.shard_map(
        shards,
        mesh=mesh,
        in_specs=placed,
        out_specs=(
            P("dp", "tm", "height", None),
            P(None, "tm", "height", None, "dp"),
            P(None, "tm", "height", None, "dp"),
            P(None, "tm", "height", None, "dp"),
        ),
        check_vma=False,
    )
```

time: 91.4 us -> 78.6 us (0.86)
  Pallas kernels: 83.6 us -> 77.1 us
  local copies, waits for them, and re-layouts: 6.03 us -> 0 us
    pallas_call x1, Pallas kernels: 83.6 us -> 75.1 us  [shards(): pl.pallas_call(kernel, out_shape=(jax.ShapeDtypeStruct((4, 256), F32), ja...]
    unnamed x23 -> x0, local copies, waits for them, and re-layouts: 4.04 us -> none
    pallas_call x0 -> x1, Pallas kernels: none -> 2.05 us  [shards(): pl.pallas_call(project, out_shape=(jax.ShapeDtypeStruct((1, 2, 2, 256), F...]
    broadcast_in_dim x2 -> x0, local copies, waits for them, and re-layouts: 1.39 us -> none  [the longest x1 0.7 us: shards(): patch_bias[None]]
where the time goes in v2:
time: 78.6 us; the launch traced here: 78.4 us
  Pallas kernels  77.1 us (98%)
  between operations  1.29 us (2%)
    pallas_call x1, Pallas kernels, shards(): pl.pallas_call(kernel, out_shape=(jax.ShapeDtypeStruct((4, 256), F32), ja...  75.1 us
    pallas_call x1, Pallas kernels, shards(): pl.pallas_call(project, out_shape=(jax.ShapeDtypeStruct((1, 2, 2, 256), F...  2.05 us

profile of v2, /device:TPU:1, one launch (start us, length us, event | category | flops | bytes accessed | tf_op | source)
XLA Modules:
  0.0 78.4 jit_solution(4486779024747344762)
XLA Ops:
  1.3 75.1 %shard_map.165 = (f32[4,256]{1,0:T(4,128)}, bf16[128,128]{1,0:T(8,128)(2,1)}, bf16[128,768]{1,0:T(8,128)(2,1)}, f32[1,768]{1,0:T(1,128)}, f32[4,16,128]{2,1,0:T(8,128)}) custom-call(bf16[2,2,16,512]{3,2,1,0:T(8,128)(2,1)} %bitcast.20, bf16[64,216]{1,0:T(8,128)(2,1)} %bitcast.21, bf16[1,64]{1,0:T(2,128)(2,1)} %bitcast.24, bf16[1,64]{1,0:T(2,128)(2,1)} %bitcast.25, ...), custom_call_target="tpu_custom_call" | custom-call | tf_op jit(solution)/shard_map/pallas_call | solution.py:803
  76.4 2.1 %shard_map.166 = (f32[1,2,2,256]{3,2,1,0:T(2,128)}, bf16[128,256]{1,0:T(8,128)(2,1)}, bf16[128,256]{1,0:T(8,128)(2,1)}, bf16[128,256]{1,0:T(8,128)(2,1)}) custom-call(f32[4,256]{1,0:T(4,128)} %get-tuple-element.13.lat_in, bf16[128,128]{1,0:T(8,128)(2,1)} %get-tuple-element.14.pat_ref, bf16[128,768]{1,0:T(8,128)(2,1)} %get-tuple-element.15.wcc_ref, ...), custom_call_target="tpu_custom_call" | custom-call | tf_op jit(solution)/shard_map/pallas_call | solution.py:889

commit v3 on v2

--- a/solution.py
+++ b/solution.py
@@ -156,9 +156,9 @@
         each(lambda k: make(k).start(), end)
         sent.append(lambda: each(lambda k: make(k).wait_send(), end))
 
-    def finish():
-        for wait in sent:
-            wait()
+    def finish(keep=0):
+        while len(sent) > keep:
+            sent.pop(0)()
 
     z_up = (lax.rem(z + 1, N), tm, hh)
     z_down = (lax.rem(z + N - 1, N), tm, hh)
@@ -347,8 +347,6 @@
             wf.at[tm], wf.at[source], wc_s.at[3, k], wc_r.at[3, k], (z, to, hh)
         )
 
-    go_each(lambda k: fold_1(k))
-
     def to_core(slot, part):
         return remote(
             part_of(xe.at[slot], part),
@@ -442,12 +440,91 @@
     ring_part(2, 1)
     for part in (2, 3):
         ring_part(1, part)
+    go_each(lambda k: fold_1(k))
     ring_part(3, 0)
     ring_part(3, 1)
     for part in (2, 3):
         ring_part(2, part)
 
-    staged[5].wait()
+    for k in (0,) + y_order:
+        for i in range(1, 4):
+            x_copy(k, i, lax.rem(x + 4 - i, 4)).wait_recv()
+        go(core_copy(k, core))
+
+    for part in (2, 3):
+        ring_part(3, part)
+
+    each(lambda k: fold_1(k).wait_recv())
+    total = wp[pl.ds(8 * tm, 8)]
+    for k in range(1, N):
+        total = total + wr[k]
+    wsum[...] = total
+    go_each(lambda k: fold_2(k))
+
+    for k in range(N):
+        core_copy(k, 1 - core).wait_recv()
+
+    def shard_of(index):
+        t, h = index // N, index % N
+        return wg[(h % 2) * 4 + t // 2, t % 2, h // 2]
+
+    for tile in range(4 * TAPS):
+        source, first = (128 * tile) // 216, (128 * tile) % 216
+        count = min(128, 216 - first)
+        value = shard_of(source)[:, first : first + count]
+        if count < 128:
+            value = jnp.concatenate([value, shard_of(source + 1)[:, : 128 - count]], axis=1)
+        tap = tile // 4
+        ij, l = tap // 3, tap % 3
+        at = 128 * (tile % 4)
+        bt[ij, 64 * l : 64 * l + 64, at : at + 128] = value
+
+    col = iota((64, 128), 1) & 15
+
+    def conv_pair(pair):
+        total = jnp.zeros((192, 128), F32)
+        for ij in range(9):
+            i, j = ij // 3, ij % 3
+            rows = [xe[2 * pair : 2 * pair + 2, i : i + 2, ROW[j + r]] for r in range(2)]
+            block = jnp.stack(rows, axis=2).reshape(128, 512)
+            total = total + lax.dot_general(bt[ij], block, NT, preferred_element_type=F32)
+        left, mid, right = total[:64], total[64:128], total[128:]
+        left = jnp.where(col == 0, left, pltpu.roll(left, 1, 1))
+        right = jnp.where(col == 15, right, pltpu.roll(right, 127, 1))
+        ht[pair] = left + mid + right
+
+    for pair in range(3):
+        core_arrived(2 * pair)
+        core_arrived(2 * pair + 1)
+        conv_pair(pair)
+    for part in range(4):
+        ring_part(4, part)
+    core_arrived(6)
+    core_arrived(7)
+    conv_pair(3)
+
+    stat_lane = iota((8, 128), 1)
+    compact = jnp.zeros((8, 128), F32)
+    for pair in range(4):
+        value = ht[pair]
+        sums = jnp.sum(value.reshape(4, 16, 128), axis=1)
+        squares = jnp.sum((value * value).reshape(4, 16, 128), axis=1)
+        both = jnp.concatenate([sums, squares], axis=0)
+        low = jnp.sum(jnp.where(stat_lane < 64, both, 0.0), axis=1, keepdims=True)
+        high = jnp.sum(jnp.where(stat_lane >= 64, both, 0.0), axis=1, keepdims=True)
+        compact = jnp.where(stat_lane == pair, low, compact)
+        compact = jnp.where(stat_lane == 64 + pair, high, compact)
+    st[0:1] = jnp.sum(pltpu.roll(compact, 0, 1, stride=4, stride_axis=0), axis=0, keepdims=True)
+
+    def stat_copy(k):
+        return remote(st.at[pl.ds(0, 1)], st.at[pl.ds(k, 1)], ss_s, ss_r, in_plane(k))
+
+    each(lambda k: stat_copy(k).start(), N * N)
+    others = st.at[pl.ds(1, N * N - 1)]
+    finish()
+
+    for copy in staged[5:]:
+        copy.wait()
     for ij in range(9):
         w2[16 * ij : 16 * ij + 16] = jnp.concatenate(
             [wo[3 * ij + l].astype(F32) for l in range(3)], axis=1
@@ -468,110 +545,6 @@
     same = ((lane & 15) == (row & 15)) & ((lane >> 8) == (row >> 6))
     place[...] = jnp.where(in_frame & in_row & same, 1.0, 0.0).astype(BF16)
 
-    for copy in staged[6:]:
-        copy.wait()
-    entry = iota((16, 128), 1) >> 1
-    token = iota((16, 128), 0)
-    is_frame = entry < 8
-    is_row = entry < 36
-    start = jnp.where(is_frame, 0, jnp.where(is_row, 8, 36))
-    width = jnp.where(is_frame, float(time_dims), float(row_dims))
-    power = 2.0 * (entry - start).astype(F32) / width
-    freq = jnp.exp(power * (-math.log(rope_base)))
-    frame_at = jnp.where(token < 8, fp_ref[0].astype(F32), fp_ref[1].astype(F32))
-    spot = jnp.where(
-        is_frame,
-        frame_at,
-        jnp.where(is_row, rp_ref[0].astype(F32), (token & 7).astype(F32)),
-    )
-    angle = spot * freq
-    odd = (iota((16, 128), 1) & 1) == 1
-    cosine = jnp.cos(angle)
-    sine = jnp.sin(angle)
-    sine = jnp.where(odd, sine, -sine)
-    for i, gain_of in enumerate((qg, kg)):
-        gain_row = jnp.broadcast_to(gain_of[...].astype(F32), (16, 128))
-        swapped = jnp.where(odd, pltpu.roll(gain_row, 1, 1), pltpu.roll(gain_row, 127, 1))
-        trig_ref[2 * i] = cosine * gain_row
-        trig_ref[2 * i + 1] = sine * swapped
-
-    for k in (0,) + y_order:
-        for i in range(1, 4):
-            x_copy(k, i, lax.rem(x + 4 - i, 4)).wait_recv()
-        go(core_copy(k, core))
-
-    for part in (2, 3):
-        ring_part(3, part)
-
-    each(lambda k: fold_1(k).wait_recv())
-    total = wp[pl.ds(8 * tm, 8)]
-    for k in range(1, N):
-        total = total + wr[k]
-    wsum[...] = total
-    go_each(lambda k: fold_2(k))
-
-    for k in range(N):
-        core_copy(k, 1 - core).wait_recv()
-
-    def shard_of(index):
-        t, h = index // N, index % N
-        return wg[(h % 2) * 4 + t // 2, t % 2, h // 2]
-
-    for tile in range(4 * TAPS):
-        source, first = (128 * tile) // 216, (128 * tile) % 216
-        count = min(128, 216 - first)
-        value = shard_of(source)[:, first : first + count]
-        if count < 128:
-            value = jnp.concatenate([value, shard_of(source + 1)[:, : 128 - count]], axis=1)
-        tap = tile // 4
-        ij, l = tap // 3, tap % 3
-        at = 128 * (tile % 4)
-        bt[ij, 64 * l : 64 * l + 64, at : at + 128] = value
-
-    col = iota((64, 128), 1) & 15
-
-    def conv_pair(pair):
-        total = jnp.zeros((192, 128), F32)
-        for ij in range(9):
-            i, j = ij // 3, ij % 3
-            rows = [xe[2 * pair : 2 * pair + 2, i : i + 2, ROW[j + r]] for r in range(2)]
-            block = jnp.stack(rows, axis=2).reshape(128, 512)
-            total = total + lax.dot_general(bt[ij], block, NT, preferred_element_type=F32)
-        left, mid, right = total[:64], total[64:128], total[128:]
-        left = jnp.where(col == 0, left, pltpu.roll(left, 1, 1))
-        right = jnp.where(col == 15, right, pltpu.roll(right, 127, 1))
-        ht[pair] = left + mid + right
-
-    for pair in range(3):
-        core_arrived(2 * pair)
-        core_arrived(2 * pair + 1)
-        conv_pair(pair)
-    for part in range(4):
-        ring_part(4, part)
-    core_arrived(6)
-    core_arrived(7)
-    conv_pair(3)
-
-    stat_lane = iota((8, 128), 1)
-    compact = jnp.zeros((8, 128), F32)
-    for pair in range(4):
-        value = ht[pair]
-        sums = jnp.sum(value.reshape(4, 16, 128), axis=1)
-        squares = jnp.sum((value * value).reshape(4, 16, 128), axis=1)
-        both = jnp.concatenate([sums, squares], axis=0)
-        low = jnp.sum(jnp.where(stat_lane < 64, both, 0.0), axis=1, keepdims=True)
-        high = jnp.sum(jnp.where(stat_lane >= 64, both, 0.0), axis=1, keepdims=True)
-        compact = jnp.where(stat_lane == pair, low, compact)
-        compact = jnp.where(stat_lane == 64 + pair, high, compact)
-    st[0, 0:1] = jnp.sum(pltpu.roll(compact, 0, 1, stride=4, stride_axis=0), axis=0, keepdims=True)
-
-    def stat_copy(k):
-        return remote(
-            st.at[0, pl.ds(0, 1)], st.at[k, pl.ds(0, 1)], ss_s.at[k], ss_r.at[k], in_plane(k)
-        )
-
-    go_each(stat_copy, N * N)
-
     each(lambda k: fold_2(k).wait_recv())
     tile_sum = wsum[hh]
     for k in range(1, N):
@@ -585,11 +558,8 @@
     diag = iota((16, 16), 0) == iota((16, 16), 1)
     out_bias = jnp.sum(jnp.where(diag, ob[...], 0.0), axis=1, keepdims=True)
 
-    each(lambda k: stat_copy(k).wait_recv(), N * N)
-    total = jnp.zeros((1, 128), F32)
-    for k in range(N * N):
-        total = total + st[k, 0:1]
-    total = jnp.broadcast_to(total, (8, 128))
+    remote(others, others, ss_s, ss_r, in_plane(1)).wait()
+    total = jnp.broadcast_to(jnp.sum(st[...], axis=0, keepdims=True), (8, 128))
     compact = pltpu.roll(total, 100, 1, stride=4, stride_axis=0)
     count = float(16 * 16 * 16 * 16)
     average = compact / count
@@ -669,6 +639,33 @@
     wf[tm] = wth[...]
     go_each(lambda k: fold_4(k, tm))
 
+    finish(7)
+
+    entry = iota((16, 128), 1) >> 1
+    token = iota((16, 128), 0)
+    is_frame = entry < 8
+    is_row = entry < 36
+    start = jnp.where(is_frame, 0, jnp.where(is_row, 8, 36))
+    width = jnp.where(is_frame, float(time_dims), float(row_dims))
+    power = 2.0 * (entry - start).astype(F32) / width
+    freq = jnp.exp(power * (-math.log(rope_base)))
+    frame_at = jnp.where(token < 8, fp_ref[0].astype(F32), fp_ref[1].astype(F32))
+    spot = jnp.where(
+        is_frame,
+        frame_at,
+        jnp.where(is_row, rp_ref[0].astype(F32), (token & 7).astype(F32)),
+    )
+    angle = spot * freq
+    odd = (iota((16, 128), 1) & 1) == 1
+    cosine = jnp.cos(angle)
+    sine = jnp.sin(angle)
+    sine = jnp.where(odd, sine, -sine)
+    for i, gain_of in enumerate((qg, kg)):
+        gain_row = jnp.broadcast_to(gain_of[...].astype(F32), (16, 128))
+        swapped = jnp.where(odd, pltpu.roll(gain_row, 1, 1), pltpu.roll(gain_row, 127, 1))
+        trig_ref[2 * i] = cosine * gain_row
+        trig_ref[2 * i + 1] = sine * swapped
+
     total = outs[0]
     for slot in range(1, N):
         rz_copy(slot).wait_recv()
@@ -719,6 +716,7 @@
         )
 
     go_each(lambda k: pb_copy(k, z))
+    finish(1)
 
     each(lambda k: fold_4(k, lax.rem(tm + N - k, N)).wait_recv())
     for lane_tile in range(6):
@@ -835,7 +833,7 @@
             pltpu.VMEM((N, 8, 128), F32),
             pltpu.VMEM((N, 8, 128), F32),
             pltpu.VMEM((N, 8, 8, 128), F32),
-            pltpu.VMEM((N * N, 8, 128), F32),
+            pltpu.VMEM((N * N, 128), F32),
             pltpu.VMEM((N, 16, 256), F32),
             pltpu.VMEM((N, 16, 256), F32),
             pltpu.VMEM((2, 16, 128), F32),
@@ -858,8 +856,8 @@
             dma((N,)),
             dma((4, N)),
             dma((4, N)),
-            dma((N * N,)),
-            dma((N * N,)),
+            dma,
+            dma,
             dma((N,)),
             dma((N,)),
             dma((5,)),

time: 78.6 us -> 75.2 us (0.957)
  Pallas kernels: 77.1 us -> 73.7 us
    pallas_call x1, Pallas kernels: 75.1 us -> 71.6 us  [shards(): pl.pallas_call(kernel, out_shape=(jax.ShapeDtypeStruct((4, 256), F32), ja...]
where the time goes in v3:
time: 75.2 us; the launch traced here: 75 us
  Pallas kernels  73.7 us (98%)
  between operations  1.29 us (2%)
    pallas_call x1, Pallas kernels, shards(): pl.pallas_call(kernel, out_shape=(jax.ShapeDtypeStruct((4, 256), F32), ja...  71.6 us
    pallas_call x1, Pallas kernels, shards(): pl.pallas_call(project, out_shape=(jax.ShapeDtypeStruct((1, 2, 2, 256), F...  2.05 us

profile of v3, /device:TPU:1, one launch (start us, length us, event | category | flops | bytes accessed | tf_op | source)
XLA Modules:
  0.0 75.0 jit_solution(5524354969934178255)
XLA Ops:
  1.3 71.6 %shard_map.165 = (f32[4,256]{1,0:T(4,128)}, bf16[128,128]{1,0:T(8,128)(2,1)}, bf16[128,768]{1,0:T(8,128)(2,1)}, f32[1,768]{1,0:T(1,128)}, f32[4,16,128]{2,1,0:T(8,128)}) custom-call(bf16[2,2,16,512]{3,2,1,0:T(8,128)(2,1)} %bitcast.20, bf16[64,216]{1,0:T(8,128)(2,1)} %bitcast.21, bf16[1,64]{1,0:T(2,128)(2,1)} %bitcast.24, bf16[1,64]{1,0:T(2,128)(2,1)} %bitcast.25, ...), custom_call_target="tpu_custom_call" | custom-call | tf_op jit(solution)/shard_map/pallas_call | solution.py:801
  72.9 2.1 %shard_map.166 = (f32[1,2,2,256]{3,2,1,0:T(2,128)}, bf16[128,256]{1,0:T(8,128)(2,1)}, bf16[128,256]{1,0:T(8,128)(2,1)}, bf16[128,256]{1,0:T(8,128)(2,1)}) custom-call(f32[4,256]{1,0:T(4,128)} %get-tuple-element.13.lat_in, bf16[128,128]{1,0:T(8,128)(2,1)} %get-tuple-element.14.pat_ref, bf16[128,768]{1,0:T(8,128)(2,1)} %get-tuple-element.15.wcc_ref, ...), custom_call_target="tpu_custom_call" | custom-call | tf_op jit(solution)/shard_map/pallas_call | solution.py:887

commit v4 on v3

--- a/solution.py
+++ b/solution.py
@@ -34,8 +34,7 @@
 
 
 def part_of(ref, which):
-    frames, rows = ((2, 0), (0, 0), (2, 2), (0, 2))[which]
-    return ref.at[pl.ds(frames, 2), pl.ds(rows, 2)]
+    return ref.at[pl.ds(0, 2), pl.ds(2 * which, 2)]
 
 
 def kernel(
@@ -59,6 +58,8 @@
     bias_ref,
     trig_ref,
     xe,
+    nx,
+    nr,
     wi,
     gg,
     gb,
@@ -94,8 +95,8 @@
     zl_r,
     ha_s,
     ha_r,
-    cc_s,
-    cc_r,
+    nx_s,
+    nx_r,
     wy_s,
     wy_r,
     wx_s,
@@ -163,8 +164,6 @@
     z_up = (lax.rem(z + 1, N), tm, hh)
     z_down = (lax.rem(z + N - 1, N), tm, hh)
     other_core = (z, tm + 1 - 2 * core, hh)
-    first_core = core == 0
-    last_core = core == 1
 
     barrier = pltpu.get_barrier_semaphore()
 
@@ -228,12 +227,8 @@
         )
 
     def z_first(part):
-        if part in (0, 2):
-            go(z_right(1, part))
-            go(z_left(1, part))
-        else:
-            go_if(first_core, lambda: z_right(1, part))
-            go_if(first_core, lambda: z_left(1, part))
+        go(z_right(1, part))
+        go(z_left(1, part))
 
     has_next = tm < N - 1
     has_last = tm > 0
@@ -242,26 +237,9 @@
     next_tm = lax.rem(tm + 1, N)
     up_h = lax.rem(hh + 1, N)
     down_h = lax.rem(hh + N - 1, N)
-    row_0 = own.at[pl.ds(2, 2), pl.ds(0, 1)]
-    row_1 = own.at[pl.ds(2, 2), pl.ds(1, 1)]
     halos = (
-        (part_of(own, 0), part_of(own, 1), (z, next_tm, hh), has_next, has_last),
-        (row_0, own.at[pl.ds(2, 2), pl.ds(3, 1)], (z, tm, down_h), has_down, has_up),
-        (row_1, own.at[pl.ds(2, 2), pl.ds(2, 1)], (z, tm, up_h), has_up, has_down),
-        (
-            row_0,
-            own.at[pl.ds(0, 2), pl.ds(3, 1)],
-            (z, next_tm, down_h),
-            last_core & has_next & has_down,
-            first_core & has_last & has_up,
-        ),
-        (
-            row_1,
-            own.at[pl.ds(0, 2), pl.ds(2, 1)],
-            (z, next_tm, up_h),
-            last_core & has_next & has_up,
-            first_core & has_last & has_down,
-        ),
+        (own.at[:, pl.ds(0, 1)], own.at[:, pl.ds(3, 1)], (z, tm, down_h), has_down, has_up),
+        (own.at[:, pl.ds(1, 1)], own.at[:, pl.ds(2, 1)], (z, tm, up_h), has_up, has_down),
     )
 
     def halo_copy(i):
@@ -271,7 +249,7 @@
     def halo_wait(i):
         pl.when(halos[i][4])(lambda: halo_copy(i).wait_recv())
 
-    for i in (3, 4, 1, 2, 0):
+    for i in range(2):
         go_if(halos[i][3], lambda i=i: halo_copy(i))
     z_first(0)
 
@@ -347,112 +325,44 @@
             wf.at[tm], wf.at[source], wc_s.at[3, k], wc_r.at[3, k], (z, to, hh)
         )
 
-    def to_core(slot, part):
-        return remote(
-            part_of(xe.at[slot], part),
-            part_of(xe.at[slot], part + 1),
-            cc_s.at[slot, part // 2],
-            cc_r.at[slot, part // 2],
-            other_core,
-        )
-
     def ring_part(step, part):
-        def pass_on():
-            z_right(step, part).wait_recv()
-            if step < 4:
-                z_right(step + 1, part).start()
-                z_left(step, part).wait_recv()
-            if step < 3:
-                z_left(step + 1, part).start()
-
-        def passed():
-            if step < 4:
-                z_right(step + 1, part).wait_send()
-            if step < 3:
-                z_left(step + 1, part).wait_send()
-
-        if part in (1, 3):
-            pl.when(first_core)(pass_on)
-            sent.append(lambda: pl.when(first_core)(passed))
-            return
-        pass_on()
-        sent.append(passed)
-        go_if(first_core, lambda: to_core(2 * step - 1, part))
+        z_right(step, part).wait_recv()
         if step < 4:
-            go_if(first_core, lambda: to_core(2 * step, part))
-
-    def core_arrived(slot):
-        @pl.when(last_core)
-        def _():
-            if slot:
-                to_core(slot, 0).wait_recv()
-            to_core(slot, 2).wait_recv()
-
+            go(z_right(step + 1, part))
+            z_left(step, part).wait_recv()
+        if step < 3:
+            go(z_left(step + 1, part))
+
+    ring_part(1, 0)
     halo_wait(0)
-
-    @pl.when(jnp.logical_not(has_last))
-    def _():
-        first = xe[0, 2:3, 0:2]
-        xe[0, 0:1, 0:2] = first
-        xe[0, 1:2, 0:2] = first
-
-    z_first(1)
-    ring_part(1, 0)
-    ring_part(1, 1)
     halo_wait(1)
-    halo_wait(2)
 
     @pl.when(jnp.logical_not(has_down))
     def _():
-        xe[0, 2:4, 2:3] = xe[0, 2:4, 0:1]
+        xe[0, :, 2:3] = xe[0, :, 0:1]
 
     @pl.when(jnp.logical_not(has_up))
     def _():
-        xe[0, 2:4, 3:4] = xe[0, 2:4, 1:2]
-
-    z_first(2)
-    go_if(first_core, lambda: to_core(0, 2))
-    halo_wait(3)
-    halo_wait(4)
-
-    @pl.when(jnp.logical_not(has_last))
-    def _():
-        first = xe[0, 2:3, 2:4]
-        xe[0, 0:1, 2:4] = first
-        xe[0, 1:2, 2:4] = first
-
-    @pl.when(first_core & has_last & jnp.logical_not(has_down))
-    def _():
-        xe[0, 0:2, 2:3] = xe[0, 0:2, 0:1]
-
-    @pl.when(first_core & has_last & jnp.logical_not(has_up))
-    def _():
-        xe[0, 0:2, 3:4] = xe[0, 0:2, 1:2]
-
-    z_first(3)
-
+        xe[0, :, 3:4] = xe[0, :, 1:2]
+
+    z_first(1)
     ring_part(2, 0)
     for k in y_order:
         y_copy(k, lax.rem(y + N - k, N)).wait_recv()
         for i in (1, 3, 2):
             go(x_copy(k, i, x))
 
-    ring_part(2, 1)
-    for part in (2, 3):
-        ring_part(1, part)
+    ring_part(1, 1)
     go_each(lambda k: fold_1(k))
     ring_part(3, 0)
-    ring_part(3, 1)
-    for part in (2, 3):
-        ring_part(2, part)
+    ring_part(2, 1)
 
     for k in (0,) + y_order:
         for i in range(1, 4):
             x_copy(k, i, lax.rem(x + 4 - i, 4)).wait_recv()
         go(core_copy(k, core))
 
-    for part in (2, 3):
-        ring_part(3, part)
+    ring_part(3, 1)
 
     each(lambda k: fold_1(k).wait_recv())
     total = wp[pl.ds(8 * tm, 8)]
@@ -481,32 +391,49 @@
 
     col = iota((64, 128), 1) & 15
 
+    late = ((iota((64, 128), 1) >> 5) & 1) == 1
+
+    def next_copy(pair):
+        return remote(
+            nx.at[pair], nr.at[pair], nx_s.at[pair], nx_r.at[pair], (z, next_tm, hh)
+        )
+
     def conv_pair(pair):
-        total = jnp.zeros((192, 128), F32)
-        for ij in range(9):
-            i, j = ij // 3, ij % 3
-            rows = [xe[2 * pair : 2 * pair + 2, i : i + 2, ROW[j + r]] for r in range(2)]
+        by_frame = [jnp.zeros((192, 128), F32) for _ in range(3)]
+        for j in range(3):
+            rows = [xe[2 * pair : 2 * pair + 2, :, ROW[j + r]] for r in range(2)]
             block = jnp.stack(rows, axis=2).reshape(128, 512)
-            total = total + lax.dot_general(bt[ij], block, NT, preferred_element_type=F32)
-        left, mid, right = total[:64], total[64:128], total[128:]
-        left = jnp.where(col == 0, left, pltpu.roll(left, 1, 1))
-        right = jnp.where(col == 15, right, pltpu.roll(right, 127, 1))
-        ht[pair] = left + mid + right
+            for i in range(3):
+                by_frame[i] = by_frame[i] + lax.dot_general(
+                    bt[3 * i + j], block, NT, preferred_element_type=F32
+                )
+        moved = []
+        for total in by_frame:
+            left, mid, right = total[:64], total[64:128], total[128:]
+            left = jnp.where(col == 0, left, pltpu.roll(left, 1, 1))
+            right = jnp.where(col == 15, right, pltpu.roll(right, 127, 1))
+            moved.append(left + mid + right)
+        two_on, one_on, same = moved
+        ht[pair] = same + jnp.where(late, pltpu.roll(one_on, 32, 1), 0.0)
+        nx[pair] = two_on + jnp.where(late, 0.0, pltpu.roll(one_on, 96, 1))
+        go_if(has_next, lambda: next_copy(pair))
+
+        @pl.when(jnp.logical_not(has_last))
+        def _():
+            nr[pair] = jnp.where(late, pltpu.roll(two_on, 32, 1), two_on + one_on)
 
     for pair in range(3):
-        core_arrived(2 * pair)
-        core_arrived(2 * pair + 1)
         conv_pair(pair)
-    for part in range(4):
+    for part in range(2):
         ring_part(4, part)
-    core_arrived(6)
-    core_arrived(7)
     conv_pair(3)
 
     stat_lane = iota((8, 128), 1)
     compact = jnp.zeros((8, 128), F32)
     for pair in range(4):
-        value = ht[pair]
+        pl.when(has_last)(lambda pair=pair: next_copy(pair).wait_recv())
+        value = ht[pair] + nr[pair]
+        ht[pair] = value
         sums = jnp.sum(value.reshape(4, 16, 128), axis=1)
         squares = jnp.sum((value * value).reshape(4, 16, 128), axis=1)
         both = jnp.concatenate([sums, squares], axis=0)
@@ -679,7 +606,13 @@
             rh.at[i],
             rh_s.at[i],
             rh_r.at[i],
-            halos[i][2],
+            (
+                (z, next_tm, hh),
+                (z, tm, down_h),
+                (z, tm, up_h),
+                (z, next_tm, down_h),
+                (z, next_tm, up_h),
+            )[i],
         )
 
     for i in range(5):
@@ -810,7 +743,9 @@
         in_specs=[hbm] * 12 + [smem] * 2,
         out_specs=(vmem,) * 5,
         scratch_shapes=[
-            pltpu.VMEM((N, 4, 4, 16, 512), BF16),
+            pltpu.VMEM((N, 2, 4, 16, 512), BF16),
+            pltpu.VMEM((4, 64, 128), F32),
+            pltpu.VMEM((4, 64, 128), F32),
             pltpu.VMEM((64, 216), BF16),
             pltpu.VMEM((1, 64), BF16),
             pltpu.VMEM((1, 64), BF16),
@@ -840,14 +775,14 @@
             pltpu.VMEM((5, 16, 128), F32),
             pltpu.VMEM((N, 16, 128), BF16),
             dma((12,)),
-            dma((4, 4)),
-            dma((4, 4)),
-            dma((3, 4)),
-            dma((3, 4)),
-            dma((5,)),
-            dma((5,)),
-            dma((N, 2)),
-            dma((N, 2)),
+            dma((4, 2)),
+            dma((4, 2)),
+            dma((3, 2)),
+            dma((3, 2)),
+            dma((2,)),
+            dma((2,)),
+            dma((4,)),
+            dma((4,)),
             dma((N,)),
             dma((N,)),
             dma((N, 4)),

time: 75.2 us -> 73.8 us (0.981)
  Pallas kernels: 73.7 us -> 72.4 us
    pallas_call x1, Pallas kernels: 71.6 us -> 70.3 us  [shards(): pl.pallas_call(kernel, out_shape=(jax.ShapeDtypeStruct((4, 256), F32), ja...]
where the time goes in v4:
time: 73.8 us; the launch traced here: 73.7 us
  Pallas kernels  72.4 us (98%)
  between operations  1.29 us (2%)
    pallas_call x1, Pallas kernels, shards(): pl.pallas_call(kernel, out_shape=(jax.ShapeDtypeStruct((4, 256), F32), ja...  70.3 us
    pallas_call x1, Pallas kernels, shards(): pl.pallas_call(project, out_shape=(jax.ShapeDtypeStruct((1, 2, 2, 256), F...  2.05 us

profile of v4, /device:TPU:1, one launch (start us, length us, event | category | flops | bytes accessed | tf_op | source)
XLA Modules:
  0.0 73.7 jit_solution(1742342640420201802)
XLA Ops:
  1.3 70.3 %shard_map.165 = (f32[4,256]{1,0:T(4,128)}, bf16[128,128]{1,0:T(8,128)(2,1)}, bf16[128,768]{1,0:T(8,128)(2,1)}, f32[1,768]{1,0:T(1,128)}, f32[4,16,128]{2,1,0:T(8,128)}) custom-call(bf16[2,2,16,512]{3,2,1,0:T(8,128)(2,1)} %bitcast.20, bf16[64,216]{1,0:T(8,128)(2,1)} %bitcast.21, bf16[1,64]{1,0:T(2,128)(2,1)} %bitcast.24, bf16[1,64]{1,0:T(2,128)(2,1)} %bitcast.25, ...), custom_call_target="tpu_custom_call" | custom-call | tf_op jit(solution)/shard_map/pallas_call | solution.py:734
  71.6 2.1 %shard_map.166 = (f32[1,2,2,256]{3,2,1,0:T(2,128)}, bf16[128,256]{1,0:T(8,128)(2,1)}, bf16[128,256]{1,0:T(8,128)(2,1)}, bf16[128,256]{1,0:T(8,128)(2,1)}) custom-call(f32[4,256]{1,0:T(4,128)} %get-tuple-element.13.lat_in, bf16[128,128]{1,0:T(8,128)(2,1)} %get-tuple-element.14.pat_ref, bf16[128,768]{1,0:T(8,128)(2,1)} %get-tuple-element.15.wcc_ref, ...), custom_call_target="tpu_custom_call" | custom-call | tf_op jit(solution)/shard_map/pallas_call | solution.py:822

commit v5 on v4

--- a/solution.py
+++ b/solution.py
@@ -165,25 +165,14 @@
     z_down = (lax.rem(z + N - 1, N), tm, hh)
     other_core = (z, tm + 1 - 2 * core, hh)
 
-    barrier = pltpu.get_barrier_semaphore()
-
-    def greet(device):
-        pl.semaphore_signal(barrier, inc=1, device_id=device, device_id_type=MESH)
-
-    def in_plane(k):
-        return (z, lax.rem(tm + k // N, N), lax.rem(hh + lax.rem(k, N), N))
-
-    each(lambda k: greet((lax.rem(z + k, N), tm, hh)))
-    each(lambda k: greet(in_plane(k)), N * N)
-
     d = tm * N + hh
     tile = jnp.minimum(48 * d // 128, 22)
     shift = 48 * d - 128 * tile
     window = pl.ds(pl.multiple_of(tile * 128, 128), 256)
     own = xe.at[0]
     staged = [
+        (x_ref, part_of(own, 0)),
         (wi_ref, wi),
-        (x_ref, part_of(own, 0)),
         (pw_ref.at[:, window], pw),
         (pb_ref, pbias),
         (qw_ref, qw),
@@ -201,11 +190,18 @@
     for copy in staged:
         copy.start()
 
-    wg[y, core, x] = jnp.zeros((64, 256), BF16)
+    barrier = pltpu.get_barrier_semaphore()
+
+    def greet(device):
+        pl.semaphore_signal(barrier, inc=1, device_id=device, device_id_type=MESH)
+
+    def in_plane(k):
+        return (z, lax.rem(tm + k // N, N), lax.rem(hh + lax.rem(k, N), N))
+
+    each(lambda k: greet((lax.rem(z + k, N), tm, hh)))
+    each(lambda k: greet(in_plane(k)), N * N)
+
     staged[0].wait()
-    wg[y, core, x, :, pl.ds(0, 216)] = wi[...]
-    staged[1].wait()
-
     pl.semaphore_wait(barrier, N - 1 + N * N - 1)
 
     def z_right(step, part):
@@ -253,6 +249,10 @@
         go_if(halos[i][3], lambda i=i: halo_copy(i))
     z_first(0)
 
+    wg[y, core, x] = jnp.zeros((64, 256), BF16)
+    staged[1].wait()
+    wg[y, core, x, :, pl.ds(0, 216)] = wi[...]
+
     def y_copy(k, source):
         return remote(
             wg.at[y, core, x],
@@ -279,10 +279,13 @@
         )
 
     y_order = (1, 7, 2, 6, 3, 5, 4)
-    for k in y_order:
-        go(y_copy(k, y))
-    for i in (1, 3, 2):
-        go(x_copy(0, i, x))
+
+    def along_x(order):
+        for k in order:
+            y_copy(k, lax.rem(y + N - k, N)).wait_recv()
+            for i in (1, 3, 2):
+                go(x_copy(k, i, x))
+
 
     for copy in staged[2:5]:
         copy.wait()
@@ -303,6 +306,11 @@
             wp[row * 6 + lane] = part[8 * row : 8 * row + 8, 128 * lane : 128 * lane + 128]
     wp[pl.ds(54, 10)] = jnp.zeros((10, 8, 128), F32)
 
+    for k in y_order:
+        go(y_copy(k, y))
+    for i in (1, 3, 2):
+        go(x_copy(0, i, x))
+
     def fold_1(k):
         to = lax.rem(tm + k, N)
         return remote(
@@ -346,12 +354,8 @@
         xe[0, :, 3:4] = xe[0, :, 1:2]
 
     z_first(1)
+    along_x(y_order)
     ring_part(2, 0)
-    for k in y_order:
-        y_copy(k, lax.rem(y + N - k, N)).wait_recv()
-        for i in (1, 3, 2):
-            go(x_copy(k, i, x))
-
     ring_part(1, 1)
     go_each(lambda k: fold_1(k))
     ring_part(3, 0)

time: 73.8 us -> 72.4 us (0.981)
  Pallas kernels: 72.4 us -> 71 us
    pallas_call x1, Pallas kernels: 70.3 us -> 68.9 us  [shards(): pl.pallas_call(kernel, out_shape=(jax.ShapeDtypeStruct((4, 256), F32), ja...]
where the time goes in v5:
time: 72.4 us; the launch traced here: 72.2 us
  Pallas kernels  71 us (98%)
  between operations  1.29 us (2%)
    pallas_call x1, Pallas kernels, shards(): pl.pallas_call(kernel, out_shape=(jax.ShapeDtypeStruct((4, 256), F32), ja...  68.9 us
    pallas_call x1, Pallas kernels, shards(): pl.pallas_call(project, out_shape=(jax.ShapeDtypeStruct((1, 2, 2, 256), F...  2.05 us

profile of v5, /device:TPU:1, one launch (start us, length us, event | category | flops | bytes accessed | tf_op | source)
XLA Modules:
  0.0 72.2 jit_solution(688656411363982375)
XLA Ops:
  1.3 68.9 %shard_map.165 = (f32[4,256]{1,0:T(4,128)}, bf16[128,128]{1,0:T(8,128)(2,1)}, bf16[128,768]{1,0:T(8,128)(2,1)}, f32[1,768]{1,0:T(1,128)}, f32[4,16,128]{2,1,0:T(8,128)}) custom-call(bf16[2,2,16,512]{3,2,1,0:T(8,128)(2,1)} %bitcast.20, bf16[64,216]{1,0:T(8,128)(2,1)} %bitcast.21, bf16[1,64]{1,0:T(2,128)(2,1)} %bitcast.24, bf16[1,64]{1,0:T(2,128)(2,1)} %bitcast.25, ...), custom_call_target="tpu_custom_call" | custom-call | tf_op jit(solution)/shard_map/pallas_call | solution.py:738
  70.2 2.1 %shard_map.166 = (f32[1,2,2,256]{3,2,1,0:T(2,128)}, bf16[128,256]{1,0:T(8,128)(2,1)}, bf16[128,256]{1,0:T(8,128)(2,1)}, bf16[128,256]{1,0:T(8,128)(2,1)}) custom-call(f32[4,256]{1,0:T(4,128)} %get-tuple-element.13.lat_in, bf16[128,128]{1,0:T(8,128)(2,1)} %get-tuple-element.14.pat_ref, bf16[128,768]{1,0:T(8,128)(2,1)} %get-tuple-element.15.wcc_ref, ...), custom_call_target="tpu_custom_call" | custom-call | tf_op jit(solution)/shard_map/pallas_call | solution.py:826

commit v6 on v5

--- a/solution.py
+++ b/solution.py
@@ -619,7 +619,7 @@
             )[i],
         )
 
-    for i in range(5):
+    for i in (3, 4, 1, 2, 0):
         go_if(goes[i], lambda i=i: rh_copy(i))
     for i in range(5):
         pl.when(comes[i])(lambda i=i: rh_copy(i).wait_recv())
@@ -652,8 +652,9 @@
             (lax.rem(z + k, N), tm, hh),
         )
 
-    go_each(lambda k: pb_copy(k, z))
-    finish(1)
+    for k in (4, 3, 5, 2, 6, 1, 7):
+        go(pb_copy(k, z))
+    finish(N - 1)
 
     each(lambda k: fold_4(k, lax.rem(tm + N - k, N)).wait_recv())
     for lane_tile in range(6):

time: 72.4 us -> 72.4 us (level)
  no operation moved by 1% of the time
where the time goes in v6:
time: 72.4 us; the launch traced here: 71.8 us
  Pallas kernels  70.5 us (97%)
  between operations  1.29 us (2%)
    pallas_call x1, Pallas kernels, shards(): pl.pallas_call(kernel, out_shape=(jax.ShapeDtypeStruct((4, 256), F32), ja...  68.5 us
    pallas_call x1, Pallas kernels, shards(): pl.pallas_call(project, out_shape=(jax.ShapeDtypeStruct((1, 2, 2, 256), F...  2.05 us

profile of v6, /device:TPU:1, one launch (start us, length us, event | category | flops | bytes accessed | tf_op | source)
XLA Modules:
  0.0 71.8 jit_solution(10837590270805760488)
XLA Ops:
  1.3 68.5 %shard_map.165 = (f32[4,256]{1,0:T(4,128)}, bf16[128,128]{1,0:T(8,128)(2,1)}, bf16[128,768]{1,0:T(8,128)(2,1)}, f32[1,768]{1,0:T(1,128)}, f32[4,16,128]{2,1,0:T(8,128)}) custom-call(bf16[2,2,16,512]{3,2,1,0:T(8,128)(2,1)} %bitcast.20, bf16[64,216]{1,0:T(8,128)(2,1)} %bitcast.21, bf16[1,64]{1,0:T(2,128)(2,1)} %bitcast.24, bf16[1,64]{1,0:T(2,128)(2,1)} %bitcast.25, ...), custom_call_target="tpu_custom_call" | custom-call | tf_op jit(solution)/shard_map/pallas_call | solution.py:739
  69.7 2.1 %shard_map.166 = (f32[1,2,2,256]{3,2,1,0:T(2,128)}, bf16[128,256]{1,0:T(8,128)(2,1)}, bf16[128,256]{1,0:T(8,128)(2,1)}, bf16[128,256]{1,0:T(8,128)(2,1)}) custom-call(f32[4,256]{1,0:T(4,128)} %get-tuple-element.13.lat_in, bf16[128,128]{1,0:T(8,128)(2,1)} %get-tuple-element.14.pat_ref, bf16[128,768]{1,0:T(8,128)(2,1)} %get-tuple-element.15.wcc_ref, ...), custom_call_target="tpu_custom_call" | custom-call | tf_op jit(solution)/shard_map/pallas_call | solution.py:827
